TPU v7x, 32 devices: a whole 2x2x4 slice. The times are simulated.
32 devices in a mesh: atoms: 16 (over z, y, core), kvec: 2 (over x).
Axes of the slice: x: 2, y: 2, z: 4, core: 2. Of those that a mesh axis runs over, the one named last changes fastest.
Arguments:
- particle_traits: bfloat16 [65536, 256], P('atoms'), may hold values from -6 to 6
- particle_coordinates: float32 [3, 65536], P(None, 'atoms'), may hold values from 0 to 24
- kspace_vectors: float32 [3, 4096], P(None, 'kvec'), may hold values from -1.5 to 1.5
- learned_kspace_filter: float32 [4096, 256], P('kvec'), may hold values from -4 to 4
- spatial_home: int32 [16, 4096], P('atoms'), may hold values from 0 to 4095, each once within a row
- following_halo_lines: int32 [16, 512], P('atoms'), may hold values from 0 to 4095
- previous_halo_lines: int32 [16, 512], P('atoms'), may hold values from 0 to 4095
- sender_projection: bfloat16 [256, 256], replicated, may hold values from -0.375 to 0.375
- receiver_projection: bfloat16 [256, 256], replicated, may hold values from -0.375 to 0.375
- pair_channel_mapping: bfloat16 [196, 256], replicated, may hold values from -0.375 to 0.375
- vertex_rescaling_gain: float32 [256], replicated, may hold values from 0.1 to 1.9
- link_sender_line: int32 [131072], P(('atoms', 'kvec')), may hold values from 0 to 5119
- link_receiver_particle: int32 [131072], P(('atoms', 'kvec')), may hold values from 0 to 4095
- active_link_tally: int32 [32], P(('atoms', 'kvec')), may hold values from 32 to 4096, as said below
Outputs:
- orbital_blocks: bfloat16 [196, 131072], P(None, ('atoms', 'kvec'))
- partitioned: bfloat16 [65536, 256], P('atoms')
Inputs may be any that keep to these rules, and one draw needn't show every extreme that they name: `spatial_home`: each row of destination orders one device's 4096 atoms; every device sends exactly 256 atoms to every partition. `following_halo_lines`: rows of the sending partition. `previous_halo_lines`: rows of the sending partition. `link_sender_line`: A table row: the partition's 4096 own atoms, then 512 ghosts from the previous partition, then 512 from the next. `active_link_tally`: A multiple of 32; the used edges are the first ones of a device's list; some device uses all 4096 slots.
All inputs are finite; a program needn't handle non-finite values.
Results may differ from a plain program's by a relative error of at most 0.01.
Values may be sent and summed in bfloat16 or wider, within the bound.
A program may use at most 64 MiB of HBM per device.

v0:
```python
import functools
import math

import jax
import jax.numpy as jnp
from jax import lax
from jax.experimental import pallas as pl
from jax.experimental.pallas import tpu as pltpu
from jax.sharding import PartitionSpec as P

F32 = jnp.float32
BF16 = jnp.bfloat16
ROUNDER = 12582912.0

def even_poly(function, count):
    nodes = [0.125 + 0.125 * math.cos(math.pi * (i + 0.5) / count) for i in range(count)]
    table = [function(u) for u in nodes]
    for level in range(1, count):
        for i in range(count - 1, level - 1, -1):
            table[i] = (table[i] - table[i - 1]) / (nodes[i] - nodes[i - level])
    coeffs = [table[-1]]
    for i in range(count - 2, -1, -1):
        shifted = [0.0] + coeffs
        scaled = [-nodes[i] * c for c in coeffs] + [0.0]
        coeffs = [a + b for a, b in zip(shifted, scaled)]
        coeffs[0] += table[i]
    return coeffs


SIN_POLY = even_poly(lambda u: math.sqrt(2.0) * math.sin(math.pi * math.sqrt(u)) / math.sqrt(u), 4)
COS_POLY = even_poly(lambda u: math.sqrt(2.0) * math.cos(math.pi * math.sqrt(u)), 4)


def horner(coeffs, u):
    total = coeffs[-1]
    for c in coeffs[-2::-1]:
        total = total * u + c
    return total


def cos_sin(turns):
    r = turns - ((turns + ROUNDER) - ROUNDER)
    u = r * r
    s = r * horner(SIN_POLY, u)
    c = horner(COS_POLY, u)
    return (1.0 - s * s).astype(BF16), (s * c).astype(BF16)


def sort_kernel(ids_ref, coords_ref, feat_ref, feat_out, coords_out):
    rows = feat_out.shape[0]
    slots = pl.program_id(0) * rows + lax.broadcasted_iota(jnp.int32, (rows, 1), 0)
    pick = jnp.where(slots == ids_ref[...], 1.0, 0.0).astype(BF16)
    feat_out[...] = jnp.dot(pick, feat_ref[...], preferred_element_type=F32).astype(BF16)
    x = coords_ref[...]
    high = x.astype(BF16).astype(F32)
    rest = x - high
    mid = rest.astype(BF16).astype(F32)
    low = rest - mid
    parts = jnp.concatenate([high, mid, low], axis=0).astype(BF16)
    moved = lax.dot_general(parts, pick, (((1,), (1,)), ((), ())), preferred_element_type=F32)
    coords_out[...] = moved[0:8] + moved[8:16] + moved[16:24]


def sort_atoms(slot_ids, coords, feat):
    a_dev, chans = feat.shape
    block = min(512, a_dev)
    padded = jnp.concatenate([coords, jnp.zeros((8 - coords.shape[0], a_dev), F32)], axis=0)
    return pl.pallas_call(
        sort_kernel,
        grid=(a_dev // block,),
        in_specs=[
            pl.BlockSpec((1, a_dev), lambda i: (0, 0)),
            pl.BlockSpec((8, a_dev), lambda i: (0, 0)),
            pl.BlockSpec((a_dev, chans), lambda i: (0, 0)),
        ],
        out_specs=[
            pl.BlockSpec((block, chans), lambda i: (i, 0)),
            pl.BlockSpec((8, block), lambda i: (0, i)),
        ],
        out_shape=[
            jax.ShapeDtypeStruct((a_dev, chans), BF16),
            jax.ShapeDtypeStruct((8, a_dev), F32),
        ],
        compiler_params=pltpu.CompilerParams(vmem_limit_bytes=48 * 1024 * 1024),
        name="sort_atoms",
    )(slot_ids, padded, feat)


def waves_kernel(chunk, k_ref, x_ref, feat_ref, cos_ref, sin_ref, sums_ref):
    rows, atoms = cos_ref.shape
    sums_ref[...] = jnp.zeros_like(sums_ref)
    strip = 16

    def one_chunk(j, carry):
        lanes = pl.ds(pl.multiple_of(j * chunk, chunk), chunk)
        x0, x1, x2 = x_ref[0:1, lanes], x_ref[1:2, lanes], x_ref[2:3, lanes]
        coses, sines = [], []
        for top in range(0, rows, strip):
            k = k_ref[top : top + strip, :]
            turns = k[:, 0:1] * x0 + k[:, 1:2] * x1 + k[:, 2:3] * x2
            c, s = cos_sin(turns)
            coses.append(c)
            sines.append(s)
        c = jnp.concatenate(coses, axis=0)
        s = jnp.concatenate(sines, axis=0)
        cos_ref[:, lanes] = c
        sin_ref[:, lanes] = s
        f = feat_ref[lanes, :]
        sums_ref[0] += jnp.dot(c, f, preferred_element_type=F32)
        sums_ref[1] += jnp.dot(s, f, preferred_element_type=F32)
        return carry

    lax.fori_loop(0, atoms // chunk, one_chunk, 0)


def waves(k_turns, coords, feat):
    kspace = k_turns.shape[0]
    a_dev, chans = feat.shape
    block = min(256, kspace)
    return pl.pallas_call(
        functools.partial(waves_kernel, min(512, a_dev)),
        grid=(kspace // block,),
        in_specs=[
            pl.BlockSpec((block, k_turns.shape[1]), lambda i: (i, 0)),
            pl.BlockSpec((8, a_dev), lambda i: (0, 0)),
            pl.BlockSpec((a_dev, chans), lambda i: (0, 0)),
        ],
        out_specs=[
            pl.BlockSpec((block, a_dev), lambda i: (i, 0)),
            pl.BlockSpec((block, a_dev), lambda i: (i, 0)),
            pl.BlockSpec((2, block, chans), lambda i: (0, i, 0)),
        ],
        out_shape=[
            jax.ShapeDtypeStruct((kspace, a_dev), BF16),
            jax.ShapeDtypeStruct((kspace, a_dev), BF16),
            jax.ShapeDtypeStruct((2, kspace, chans), F32),
        ],
        compiler_params=pltpu.CompilerParams(vmem_limit_bytes=48 * 1024 * 1024),
        cost_estimate=pl.CostEstimate(
            flops=60 * kspace * a_dev + 4 * kspace * a_dev * chans,
            bytes_accessed=4 * kspace * a_dev,
            transcendentals=0,
        ),
        name="waves",
    )(k_turns, coords, feat)


def update_kernel(filt_ref, cos_ref, sin_ref, out_ref, turned):
    @pl.when(pl.program_id(0) == 0)
    def _():
        turned[0] = filt_ref[0].astype(F32).T.astype(BF16)
        turned[1] = filt_ref[1].astype(F32).T.astype(BF16)

    total = jnp.dot(turned[0], cos_ref[...], preferred_element_type=F32)
    total = total + jnp.dot(turned[1], sin_ref[...], preferred_element_type=F32)
    out_ref[...] = total.T.astype(BF16)


def update_rows(filt, cosine, sine):
    kspace, a_dev = cosine.shape
    chans = filt.shape[2]
    block = min(512, a_dev)
    return pl.pallas_call(
        update_kernel,
        grid=(a_dev // block,),
        in_specs=[
            pl.BlockSpec((2, kspace, chans), lambda i: (0, 0, 0)),
            pl.BlockSpec((kspace, block), lambda i: (0, i)),
            pl.BlockSpec((kspace, block), lambda i: (0, i)),
        ],
        out_specs=pl.BlockSpec((block, chans), lambda i: (i, 0)),
        out_shape=jax.ShapeDtypeStruct((a_dev, chans), BF16),
        scratch_shapes=[pltpu.VMEM((2, chans, kspace), BF16)],
        compiler_params=pltpu.CompilerParams(vmem_limit_bytes=48 * 1024 * 1024),
        cost_estimate=pl.CostEstimate(
            flops=4 * kspace * a_dev * chans, bytes_accessed=4 * kspace * a_dev, transcendentals=0
        ),
        name="update_rows",
    )(filt, cosine, sine)


def edges_kernel(src_ref, dst_ref, used_ref, table_ref, own_ref, send_ref, recv_ref, map_ref, out_ref, left, right, pair):
    step = pl.program_id(0)
    block = pair.shape[0]
    strip = 512

    @pl.when(step == 0)
    def _():
        def project(source, weight, target):
            def one(i, carry):
                rows = pl.ds(pl.multiple_of(i * strip, strip), strip)
                found = jnp.dot(source[rows, :], weight[...], preferred_element_type=F32)
                target[rows, :] = found.astype(BF16).astype(F32)
                return carry

            lax.fori_loop(0, source.shape[0] // strip, one, 0)

        project(table_ref, send_ref, left)
        project(own_ref, recv_ref, right)

    first = step * block
    used = used_ref[0]

    @pl.when(first < used)
    def _():
        def eight(i, carry):
            at = pl.multiple_of(i * 8, 8)
            rows = []
            for n in range(8):
                e = first + at + n
                rows.append(left[pl.ds(src_ref[e], 1), :] * right[pl.ds(dst_ref[e], 1), :])
            pair[pl.ds(at, 8), :] = jnp.concatenate(rows, axis=0)
            return carry

        lax.fori_loop(0, block // 8, eight, 0)
        orb = lax.dot_general(
            map_ref[...], pair[...].astype(BF16), (((1,), (1,)), ((), ())), preferred_element_type=F32
        )
        slots = first + lax.broadcasted_iota(jnp.int32, (1, block), 1)
        out_ref[...] = jnp.where(slots < used, orb, 0.0).astype(BF16)

    @pl.when(first >= used)
    def _():
        out_ref[...] = jnp.zeros_like(out_ref)


def edges(src, dst, used, table, own, send_w, recv_w, mapping):
    e_dev = src.shape[0]
    orbitals, chans = mapping.shape
    block = min(512, e_dev)
    whole = pl.BlockSpec(memory_space=pltpu.VMEM)
    scalars = pl.BlockSpec(memory_space=pltpu.SMEM)
    return pl.pallas_call(
        edges_kernel,
        grid=(e_dev // block,),
        in_specs=[scalars, scalars, scalars, whole, whole, whole, whole, whole],
        out_specs=pl.BlockSpec((orbitals, block), lambda i: (0, i)),
        out_shape=jax.ShapeDtypeStruct((orbitals, e_dev), BF16),
        scratch_shapes=[
            pltpu.VMEM((table.shape[0], chans), F32),
            pltpu.VMEM((own.shape[0], chans), F32),
            pltpu.VMEM((block, chans), F32),
        ],
        compiler_params=pltpu.CompilerParams(vmem_limit_bytes=48 * 1024 * 1024),
        name="edges",
    )(src, dst, used, table, own, send_w, recv_w, mapping)


def from_behind(array, axis, by):
    devices = lax.axis_size(axis)
    return lax.ppermute(array, axis, [(i, (i + by) % devices) for i in range(devices)])


def strides(devices):
    found, stride = [], 1
    for size in (2, 2):
        if devices % (stride * size) == 0 and devices > stride:
            found.append((stride, size))
            stride *= size
    if devices > stride:
        found.append((stride, devices // stride))
    return found


def shifted(array, devices, stride, size, by):
    pairs = []
    for i in range(devices):
        place = (i // stride) % size
        pairs.append((i, i + ((place + by) % size - place) * stride))
    return lax.ppermute(array, "atoms", pairs)


def scatter_sum(array, dim):
    devices = lax.axis_size("atoms")
    me = lax.axis_index("atoms")
    array = array.astype(BF16)
    for stride, size in strides(devices):
        place = (me // stride) % size
        part = array.shape[dim] // size
        total = lax.dynamic_slice_in_dim(array, place * part, part, dim).astype(F32)
        for by in range(1, size):
            away = lax.rem(place + by, size)
            piece = lax.dynamic_slice_in_dim(array, away * part, part, dim)
            total = total + shifted(piece, devices, stride, size, by).astype(F32)
        array = total.astype(BF16)
    return total


def part_start(total):
    devices = lax.axis_size("atoms")
    me = lax.axis_index("atoms")
    start = 0
    for stride, size in strides(devices):
        total = total // size
        start = start + ((me // stride) % size) * total
    return start


def gather_parts(array, dim):
    devices = lax.axis_size("atoms")
    me = lax.axis_index("atoms")
    for stride, size in reversed(strides(devices)):
        place = (me // stride) % size
        part = array.shape[dim]
        shape = list(array.shape)
        shape[dim] = part * size
        whole = lax.dynamic_update_slice_in_dim(jnp.zeros(shape, array.dtype), array, place * part, dim)
        for by in range(1, size):
            came = lax.rem(place - by + size, size)
            moved = shifted(array, devices, stride, size, by)
            whole = lax.dynamic_update_slice_in_dim(whole, moved, came * part, dim)
        array = whole
    return array


def finish_rows(feat_rows, update, gain):
    refreshed = feat_rows.astype(F32) + jax.nn.silu(update)
    scaled = refreshed * lax.rsqrt(jnp.mean(refreshed * refreshed, axis=-1, keepdims=True) + 1e-06)
    return (scaled * gain).astype(BF16)


def local(
    particle_traits,
    particle_coordinates,
    kspace_vectors,
    learned_kspace_filter,
    spatial_home,
    following_halo_lines,
    previous_halo_lines,
    sender_projection,
    receiver_projection,
    pair_channel_mapping,
    vertex_rescaling_gain,
    link_sender_line,
    link_receiver_particle,
    active_link_tally,
):
    n_atoms = lax.axis_size("atoms")
    kspace_tally = lax.axis_size("kvec")
    a_dev, chans = particle_traits.shape
    group = a_dev // n_atoms
    sub_rows = group // kspace_tally
    kspace = kspace_vectors.shape[1]
    norm_scale = 1.0 / math.sqrt(a_dev * n_atoms * kspace * kspace_tally)

    sorted_feat, sorted_coords = sort_atoms(spatial_home, particle_coordinates, particle_traits)
    k_turns = (kspace_vectors * (0.5 / math.pi)).T
    cosine, sine, sums = waves(k_turns, sorted_coords, sorted_feat)
    mine = scatter_sum(sums, 1)
    own_filter = lax.dynamic_slice_in_dim(learned_kspace_filter, part_start(kspace), kspace // n_atoms, 0)
    filt = (own_filter[None] * mine * norm_scale).astype(BF16)
    filt = gather_parts(filt, 1)
    partial = update_rows(filt, cosine, sine).reshape(n_atoms, group, chans)

    kvec_index = lax.axis_index("kvec")
    update_share = lax.dynamic_slice_in_dim(partial, kvec_index * sub_rows, sub_rows, 1).astype(F32)
    for by in range(1, kspace_tally):
        away = lax.rem(kvec_index + by, kspace_tally)
        piece = lax.dynamic_slice_in_dim(partial, away * sub_rows, sub_rows, 1)
        update_share = update_share + from_behind(piece, "kvec", by).astype(F32)
    feat_share = lax.dynamic_slice_in_dim(
        sorted_feat.reshape(n_atoms, group, chans), kvec_index * sub_rows, sub_rows, 1
    )
    node_share = finish_rows(feat_share, update_share, vertex_rescaling_gain)
    arrived = lax.all_to_all(node_share, "atoms", split_axis=0, concat_axis=0, tiled=True)
    gathered = lax.all_gather(arrived, "kvec", axis=1, tiled=True)
    partition_rows = gathered.reshape(a_dev, chans)
    from_lower = from_behind(partition_rows[following_halo_lines[0]], "atoms", 1)
    from_upper = from_behind(partition_rows[previous_halo_lines[0]], "atoms", -1)
    row_table = jnp.concatenate([partition_rows, from_lower, from_upper], axis=0)
    orbital_blocks = edges(
        link_sender_line,
        link_receiver_particle,
        active_link_tally,
        row_table,
        partition_rows,
        sender_projection,
        receiver_projection,
        pair_channel_mapping,
    )
    return (orbital_blocks, partition_rows)


def solution(mesh):
    placed = (
        P("atoms", None),
        P(None, "atoms"),
        P(None, "kvec"),
        P("kvec", None),
        P("atoms", None),
        P("atoms", None),
        P("atoms", None),
        P(),
        P(),
        P(),
        P(),
        P(("atoms", "kvec")),
        P(("atoms", "kvec")),
        P(("atoms", "kvec")),
    )
    return jax.shard_map(
        local,
        mesh=mesh,
        in_specs=placed,
        out_specs=(P(None, ("atoms", "kvec")), P("atoms", None)),
        check_vma=False,
    )
```

profile of v0, /device:TPU:23, one launch (start us, length us, event | category | flops | bytes accessed | tf_op | source)
XLA Modules:
  0.0 302.7 jit_solution(604476068715987400)
XLA Ops:
  9.4 1.6 copy-done.4
  11.7 18.7 %sort_atoms.1 = (bf16[4096,256]{1,0:T(8,128)(2,1)S(1)}, f32[8,4096]{1,0:T(8,128)S(1)}) custom-call(s32[1,4096]{1,0:T(1,128)S(1)} %copy-done.9, f32[8,4096]{1,0:T(8,128)S(1)} %concatenate.6.coords_ref, bf16[4096,256]{1,0:T(8,128)(2,1)S(1)} %copy-done.4), custom_call_target="tpu_custom_call" | custom-call | tf_op jit(solution)/shard_map/sort_atoms/pallas_call | solution.py:68
  30.4 44.6 %waves.1 = (bf16[2048,4096]{1,0:T(8,128)(2,1)}, bf16[2048,4096]{1,0:T(8,128)(2,1)}, f32[2,2048,256]{2,1,0:T(8,128)}) custom-call(f32[2048,3]{1,0:T(8,128)S(1)} %bitcast.17, f32[8,4096]{1,0:T(8,128)S(1)} %get-tuple-element.8.x_ref, bf16[4096,256]{1,0:T(8,128)(2,1)S(1)} %get-tuple-element.7.feat_ref), custom_call_target="tpu_custom_call" | custom-call | flops 9093251072 | bytes 33554432 | tf_op jit(solution)/shard_map/waves/pallas_call | solution.py:120
  75.0 3.7 %convert_element_type.49 = bf16[2,2048,256]{2,1,0:T(8,128)(2,1)} convert(f32[2,2048,256]{2,1,0:T(8,128)} %get-tuple-element.9) | non-fusion elementwise | flops 1048576 | bytes 6291456 | tf_op jit(solution)/shard_map/convert_element_type | solution.py:276
  78.7 1.3 constant_dynamic-slice_fusion.5
  80.7 2.4 collective-permute-done
  83.2 1.8 add_convert_fusion
  86.0 13.2 %collective-permute-done.1 = bf16[2,512,256]{2,1,0:T(8,128)(2,1)} collective-permute-done((bf16[2,512,256]{2,1,0:T(8,128)(2,1)}, bf16[2,512,256]{2,1,0:T(8,128)(2,1)}, u32[]{:S(2)}, u32[]{:S(2)}) %collective-permute-start.1) | collective-permute-done | bytes 524320 | tf_op jit(solution)/shard_map/ppermute | solution.py:270
  99.3 1.2 add_convert_fusion.1
  101.3 1.4 collective-permute-start.2
  102.7 1.2 collective-permute-start.4
  103.9 1.2 collective-permute-done.2
  105.1 6.0 %collective-permute-done.3 = bf16[2,128,256]{2,1,0:T(8,128)(2,1)S(1)} collective-permute-done((bf16[2,128,256]{2,1,0:T(8,128)(2,1)S(1)}, bf16[2,128,256]{2,1,0:T(8,128)(2,1)S(1)}, u32[]{:S(2)}, u32[]{:S(2)}) %collective-permute-start.3) | collective-permute-done | bytes 131104 | tf_op jit(solution)/shard_map/ppermute | solution.py:270
  111.2 2.8 collective-permute-done.4
  115.5 2.9 collective-permute-start.6
  118.5 2.2 collective-permute-done.5
  120.7 4.5 %collective-permute-done.6 = bf16[2,128,256]{2,1,0:T(8,128)(2,1)S(1)} collective-permute-done((bf16[2,128,256]{2,1,0:T(8,128)(2,1)S(1)}, bf16[2,128,256]{2,1,0:T(8,128)(2,1)S(1)}, u32[]{:S(2)}, u32[]{:S(2)}) %collective-permute-start.6) | collective-permute-done | bytes 131104 | tf_op jit(solution)/shard_map/ppermute | solution.py:270
  125.3 2.8 collective-permute-done.7
  128.5 12.6 %collective-permute-done.8 = bf16[2,512,256]{2,1,0:T(8,128)(2,1)S(1)} collective-permute-done((bf16[2,512,256]{2,1,0:T(8,128)(2,1)S(1)}, bf16[2,512,256]{2,1,0:T(8,128)(2,1)S(1)}, u32[]{:S(2)}, u32[]{:S(2)}) %collective-permute-start.8) | collective-permute-done | bytes 524320 | tf_op jit(solution)/shard_map/ppermute | solution.py:270
  141.2 1.4 collective-permute-start.9
  142.8 2.1 collective-permute-done.9
  145.0 16.7 %update_rows.1 = bf16[4096,256]{1,0:T(8,128)(2,1)S(1)} custom-call(bf16[2,2048,256]{2,1,0:T(8,128)(2,1)S(1)} %constant_dynamic-update-slice_fusion.filt_ref, bf16[2048,4096]{1,0:T(8,128)(2,1)} %get-tuple-element.10.cos_ref, bf16[2048,4096]{1,0:T(8,128)(2,1)} %get-tuple-element.11.sin_ref), custom_call_target="tpu_custom_call" | custom-call | flops 8589934592 | bytes 33554432 | tf_op jit(solution)/shard_map/update_rows/pallas_call | solution.py:163
  162.1 24.2 %collective-permute-done.10 = bf16[16,128,256]{2,1,0:T(8,128)(2,1)} collective-permute-done((bf16[16,128,256]{2,1,0:T(8,128)(2,1)S(1)}, bf16[16,128,256]{2,1,0:T(8,128)(2,1)}, u32[]{:S(2)}, u32[]{:S(2)}) %collective-permute-start.10) | collective-permute-done | bytes 1048608 | tf_op jit(solution)/shard_map/ppermute | solution.py:251
  186.3 2.5 multiply_reduce_fusion
  189.2 30.9 %all_to_all.5 = bf16[16,128,256]{2,1,0:T(8,128)(2,1)} all-to-all(bf16[16,128,256]{2,1,0:T(8,128)(2,1)S(1)} %multiply_convert_fusion), channel_id=1, replica_groups=mesh['atoms'=16,'kvec'=2] {'atoms'}, dimensions={0} | all-to-all | bytes 2097152 | tf_op jit(solution)/shard_map/all_to_all | solution.py:365
  220.1 33.7 %all-gather.2.cloned.1.call-done = bf16[16,256,256]{2,1,0:T(8,128)(2,1)} async-done(((bf16[16,128,256]{2,1,0:T(8,128)(2,1)}), bf16[16,256,256]{2,1,0:T(8,128)(2,1)}) %all-gather.2.cloned.1.call-update) | async-done | bytes 2097168 | tf_op jit(solution)/shard_map/all_gather | solution.py:366
  253.8 3.6 %gather_fusion = bf16[512,256]{1,0:T(8,128)(2,1)S(1)} fusion(bf16[4096,256]{1,0:T(8,128)(2,1)} %bitcast.10, s32[1024]{0:T(1024)S(1)} %pad_clamp_fusion.1), kind=kCustom, calls=%fused_computation | custom fusion | bytes 526336 | tf_op jit(solution)/shard_map/gather | solution.py:368
  257.4 1.8 collective-permute-start.11
  259.2 1.9 gather_fusion.1
  262.5 5.4 %collective-permute-done.12 = bf16[512,256]{1,0:T(8,128)(2,1)S(1)} collective-permute-done((bf16[512,256]{1,0:T(8,128)(2,1)S(1)}, bf16[512,256]{1,0:T(8,128)(2,1)S(1)}, u32[]{:S(2)}, u32[]{:S(2)}) %collective-permute-start.12) | collective-permute-done | bytes 262176 | tf_op jit(solution)/shard_map/ppermute | solution.py:251
  268.1 26.4 %edges.1 = bf16[196,4096]{1,0:T(8,128)(2,1)} custom-call(s32[4096]{0:T(1024)S(1)} %copy-done.10, s32[4096]{0:T(1024)S(1)} %copy-done.11, s32[1]{0:T(128)S(6)} %copy.30.used_ref, bf16[5120,256]{1,0:T(8,128)(2,1)S(1)} %pad_maximum_fusion.table_ref, bf16[4096,256]{1,0:T(8,128)(2,1)S(1)} %bitcast.13, bf16[256,256]{1,0:T(8,128)(2,1)S(1)} %copy-done.6, ...), custom_call_target="tpu_custom_call" | custom-call | tf_op jit(solution)/shard_map/edges/pallas_call | solution.py:233
  294.5 1.3 copy.31
  (66 shorter events, 9.6 us)
Async XLA Ops:
  7.2 96.7 %copy-start = (f32[2048,256]{1,0:T(8,128)S(1)}, f32[2048,256]{1,0:T(8,128)}, u32[]{:S(2)}) copy-start(f32[2048,256]{1,0:T(8,128)} %param.17) | copy-start | bytes 6291460
  7.2 246.6 %all-gather.2.cloned.1.call-start = ((), (), s32[]{:S(2)}) async-start(), calls=%async_computation.1 | async-start | bytes 3145728 | tf_op jit(solution)/shard_map/all_gather | solution.py:366
  9.4 1.6 copy-start.4
  11.0 0.7 copy-start.9
  30.4 44.6 %copy-start.5 = (bf16[4096,256]{1,0:T(8,128)(2,1)}, bf16[4096,256]{1,0:T(8,128)(2,1)S(1)}, u32[]{:S(2)}) copy-start(bf16[4096,256]{1,0:T(8,128)(2,1)S(1)} %get-tuple-element.7.feat_ref) | copy-start | bytes 6291460
  80.0 3.2 %collective-permute-start = (bf16[2,1024,256]{2,1,0:T(8,128)(2,1)S(1)}, bf16[2,1024,256]{2,1,0:T(8,128)(2,1)}, u32[]{:S(2)}, u32[]{:S(2)}) collective-permute-start(bf16[2,1024,256]{2,1,0:T(8,128)(2,1)S(1)} %constant_dynamic-slice_fusion.5), channel_id=1, source_target_pairs={{0,2},{2,0},{4,6},{6,4},{8,10},{10,8},{12,14},{14,12},{16,18},{18,... | collective-permute-start | bytes 3145736 | tf_op jit(solution)/shard_map/ppermute | solution.py:270
  85.8 13.5 %collective-permute-start.1 = (bf16[2,512,256]{2,1,0:T(8,128)(2,1)}, bf16[2,512,256]{2,1,0:T(8,128)(2,1)}, u32[]{:S(2)}, u32[]{:S(2)}) collective-permute-start(bf16[2,512,256]{2,1,0:T(8,128)(2,1)} %constant_dynamic-slice_fusion.4), channel_id=1, source_target_pairs={{0,4},{2,6},{4,0},{6,2},{8,12},{10,14},{12,8},{14,10},{16,20},{18,... | collective-permute-start | bytes 1572872 | tf_op jit(solution)/shard_map/ppermute | solution.py:270
  100.4 0.8 copy-start.12
  101.3 3.9 %collective-permute-start.2 = (bf16[2,128,256]{2,1,0:T(8,128)(2,1)S(1)}, bf16[2,128,256]{2,1,0:T(8,128)(2,1)S(1)}, u32[]{:S(2)}, u32[]{:S(2)}) collective-permute-start(bf16[2,128,256]{2,1,0:T(8,128)(2,1)S(1)} %get-tuple-element.16), channel_id=1, source_target_pairs={{0,8},{2,10},{4,12},{6,14},{8,16},{10,18},{12,20},{14,22},{16,24},... | collective-permute-start | bytes 393224 | tf_op jit(solution)/shard_map/ppermute | solution.py:270
  102.6 8.6 %collective-permute-start.3 = (bf16[2,128,256]{2,1,0:T(8,128)(2,1)S(1)}, bf16[2,128,256]{2,1,0:T(8,128)(2,1)S(1)}, u32[]{:S(2)}, u32[]{:S(2)}) collective-permute-start(bf16[2,128,256]{2,1,0:T(8,128)(2,1)S(1)} %get-tuple-element.18), channel_id=1, source_target_pairs={{0,16},{2,18},{4,20},{6,22},{8,24},{10,26},{12,28},{14,30},{16,0},... | collective-permute-start | bytes 393224 | tf_op jit(solution)/shard_map/ppermute | solution.py:270
  102.7 11.3 %collective-permute-start.4 = (bf16[2,128,256]{2,1,0:T(8,128)(2,1)S(1)}, bf16[2,128,256]{2,1,0:T(8,128)(2,1)S(1)}, u32[]{:S(2)}, u32[]{:S(2)}) collective-permute-start(bf16[2,128,256]{2,1,0:T(8,128)(2,1)S(1)} %get-tuple-element.17), channel_id=1, source_target_pairs={{0,24},{2,26},{4,28},{6,30},{8,0},{10,2},{12,4},{14,6},{16,8},{18,... | collective-permute-start | bytes 393224 | tf_op jit(solution)/shard_map/ppermute | solution.py:270
  115.0 5.7 %collective-permute-start.5 = (bf16[2,128,256]{2,1,0:T(8,128)(2,1)S(1)}, bf16[2,128,256]{2,1,0:T(8,128)(2,1)S(1)}, u32[]{:S(2)}, u32[]{:S(2)}) collective-permute-start(bf16[2,128,256]{2,1,0:T(8,128)(2,1)S(1)} %get-tuple-element.15), channel_id=1, source_target_pairs={{0,8},{2,10},{4,12},{6,14},{8,16},{10,18},{12,20},{14,22},{16,24},... | collective-permute-start | bytes 393224 | tf_op jit(solution)/shard_map/ppermute | solution.py:270
  115.5 9.8 %collective-permute-start.6 = (bf16[2,128,256]{2,1,0:T(8,128)(2,1)S(1)}, bf16[2,128,256]{2,1,0:T(8,128)(2,1)S(1)}, u32[]{:S(2)}, u32[]{:S(2)}) collective-permute-start(bf16[2,128,256]{2,1,0:T(8,128)(2,1)S(1)} %get-tuple-element.15), channel_id=1, source_target_pairs={{0,16},{2,18},{4,20},{6,22},{8,24},{10,26},{12,28},{14,30},{16,0},... | collective-permute-start | bytes 393224 | tf_op jit(solution)/shard_map/ppermute | solution.py:270
  118.5 9.6 %collective-permute-start.7 = (bf16[2,128,256]{2,1,0:T(8,128)(2,1)S(1)}, bf16[2,128,256]{2,1,0:T(8,128)(2,1)S(1)}, u32[]{:S(2)}, u32[]{:S(2)}) collective-permute-start(bf16[2,128,256]{2,1,0:T(8,128)(2,1)S(1)} %get-tuple-element.15), channel_id=1, source_target_pairs={{0,24},{2,26},{4,28},{6,30},{8,0},{10,2},{12,4},{14,6},{16,8},{18,... | collective-permute-start | bytes 393224 | tf_op jit(solution)/shard_map/ppermute | solution.py:270
  128.1 13.1 %collective-permute-start.8 = (bf16[2,512,256]{2,1,0:T(8,128)(2,1)S(1)}, bf16[2,512,256]{2,1,0:T(8,128)(2,1)S(1)}, u32[]{:S(2)}, u32[]{:S(2)}) collective-permute-start(bf16[2,512,256]{2,1,0:T(8,128)(2,1)S(1)} %constant_dynamic-update-slice_fusion.4), channel_id=1, source_target_pairs={{0,4},{2,6},{4,0},{6,2},{8,12},{10,14},{12,8},{14,10},{16,20},{18,... | collective-permute-start | bytes 1572872 | tf_op jit(solution)/shard_map/ppermute | solution.py:270
  141.2 3.7 %collective-permute-start.9 = (bf16[2,1024,256]{2,1,0:T(8,128)(2,1)S(1)}, bf16[2,1024,256]{2,1,0:T(8,128)(2,1)S(1)}, u32[]{:S(2)}, u32[]{:S(2)}) collective-permute-start(bf16[2,1024,256]{2,1,0:T(8,128)(2,1)S(1)} %constant_dynamic-update-slice_fusion.2), channel_id=1, source_target_pairs={{0,2},{2,0},{4,6},{6,4},{8,10},{10,8},{12,14},{14,12},{16,18},{18,... | collective-permute-start | bytes 3145736 | tf_op jit(solution)/shard_map/ppermute | solution.py:270
  161.8 24.5 %collective-permute-start.10 = (bf16[16,128,256]{2,1,0:T(8,128)(2,1)S(1)}, bf16[16,128,256]{2,1,0:T(8,128)(2,1)}, u32[]{:S(2)}, u32[]{:S(2)}) collective-permute-start(bf16[16,128,256]{2,1,0:T(8,128)(2,1)S(1)} %constant_dynamic-slice_fusion), channel_id=1, source_target_pairs={{0,1},{1,0},{2,3},{3,2},{4,5},{5,4},{6,7},{7,6},{8,9},{9,8},{10,11... | collective-permute-start | bytes 3145736 | tf_op jit(solution)/shard_map/ppermute | solution.py:251
  186.3 2.5 copy-start.15
  189.1 30.9 %copy-start.13 = (s32[1,512]{1,0:T(1,128)S(1)}, s32[1,512]{1,0:T(1,128)}, u32[]{:S(2)}) copy-start(s32[1,512]{1,0:T(1,128)} %param.20) | copy-start | bytes 6148
  189.1 30.9 %copy-start.14 = (s32[1,512]{1,0:T(1,128)S(1)}, s32[1,512]{1,0:T(1,128)}, u32[]{:S(2)}) copy-start(s32[1,512]{1,0:T(1,128)} %param.19) | copy-start | bytes 6148
  253.8 5.4 %copy-start.2 = (bf16[16,256,256]{2,1,0:T(8,128)(2,1)S(1)}, bf16[16,256,256]{2,1,0:T(8,128)(2,1)}, u32[]{:S(2)}) copy-start(bf16[16,256,256]{2,1,0:T(8,128)(2,1)} %all-gather.2.cloned.1.call-done) | copy-start | bytes 6291460
  257.4 5.1 %collective-permute-start.11 = (bf16[512,256]{1,0:T(8,128)(2,1)S(1)}, bf16[512,256]{1,0:T(8,128)(2,1)S(1)}, u32[]{:S(2)}, u32[]{:S(2)}) collective-permute-start(bf16[512,256]{1,0:T(8,128)(2,1)S(1)} %gather_fusion), channel_id=1, source_target_pairs={{0,2},{2,4},{4,6},{6,8},{8,10},{10,12},{12,14},{14,16},{16,18},{18... | collective-permute-start | bytes 786440 | tf_op jit(solution)/shard_map/ppermute | solution.py:251
  261.1 6.7 %collective-permute-start.12 = (bf16[512,256]{1,0:T(8,128)(2,1)S(1)}, bf16[512,256]{1,0:T(8,128)(2,1)S(1)}, u32[]{:S(2)}, u32[]{:S(2)}) collective-permute-start(bf16[512,256]{1,0:T(8,128)(2,1)S(1)} %gather_fusion.1), channel_id=1, source_target_pairs={{0,30},{2,0},{4,2},{6,4},{8,6},{10,8},{12,10},{14,12},{16,14},{18,... | collective-permute-start | bytes 786440 | tf_op jit(solution)/shard_map/ppermute | solution.py:251
  261.9 6.2 %copy-start.3 = (bf16[16,256,256]{2,1,0:T(8,128)(2,1)S(1)}, bf16[16,256,256]{2,1,0:T(8,128)(2,1)}, u32[]{:S(2)}) copy-start(bf16[16,256,256]{2,1,0:T(8,128)(2,1)} %all-gather.2.cloned.1.call-done) | copy-start | bytes 6291460
  261.9 6.2 %copy-start.6 = (bf16[256,256]{1,0:T(8,128)(2,1)S(1)}, bf16[256,256]{1,0:T(8,128)(2,1)}, u32[]{:S(2)}) copy-start(bf16[256,256]{1,0:T(8,128)(2,1)} %send_ref.1) | copy-start | bytes 393220
  261.9 6.2 %copy-start.7 = (bf16[256,256]{1,0:T(8,128)(2,1)S(1)}, bf16[256,256]{1,0:T(8,128)(2,1)}, u32[]{:S(2)}) copy-start(bf16[256,256]{1,0:T(8,128)(2,1)} %recv_ref.1) | copy-start | bytes 393220
  261.9 6.2 %copy-start.8 = (bf16[196,256]{1,0:T(8,128)(2,1)S(1)}, bf16[196,256]{1,0:T(8,128)(2,1)}, u32[]{:S(2)}) copy-start(bf16[196,256]{1,0:T(8,128)(2,1)} %map_ref.1) | copy-start | bytes 301060
  261.9 6.2 %copy-start.10 = (s32[4096]{0:T(1024)S(1)}, s32[4096]{0:T(1024)}, u32[]{:S(2)}) copy-start(s32[4096]{0:T(1024)} %src_ref.1) | copy-start | bytes 49156
  261.9 6.2 %copy-start.11 = (s32[4096]{0:T(1024)S(1)}, s32[4096]{0:T(1024)}, u32[]{:S(2)}) copy-start(s32[4096]{0:T(1024)} %dst_ref.1) | copy-start | bytes 49156
  268.1 27.7 %copy-start.1 = (f32[2048,256]{1,0:T(8,128)S(1)}, f32[2048,256]{1,0:T(8,128)}, u32[]{:S(2)}) copy-start(f32[2048,256]{1,0:T(8,128)} %param.17) | copy-start | bytes 6291460
Sparse Core Ops, SparseCore 0:
  220.2 33.5 all-gather.1
where the time goes:
time: 305 us; the launch traced here: 303 us
  waiting for transfers between devices  114 us (37%)
  Pallas kernels  106 us (35%)
  blocking collectives  30.9 us (10%)
  between operations  15 us (5%)
  local copies, waits for them, and re-layouts  14 us (5%)
  other arithmetic  11.6 us (4%)
  starting transfers between devices  10.9 us (4%)
    ppermute x10, waiting for transfers between devices, shifted(): return lax.ppermute(array, 'atoms', pairs)  50 us
    pallas_call x1, Pallas kernels, waves(): pl.pallas_call(functools.partial(waves_kernel, min(512, a_dev)), grid=(ks...  44.6 us
    all_gather x1, waiting for transfers between devices, local(): gathered = lax.all_gather(arrived, 'kvec', axis=1, tiled=True)  33.7 us
    all_to_all x1, blocking collectives, local(): lax.all_to_all(node_share, 'atoms', split_axis=0, concat_axis=0, tiled=True)  30.9 us
    ppermute x3, waiting for transfers between devices, from_behind(): lax.ppermute(array, axis, [(i, (i + by) % devices) for i in range(devices)])  30.2 us
    pallas_call x1, Pallas kernels, edges(): pl.pallas_call(edges_kernel, grid=(e_dev // block,), in_specs=[scalars, s...  26.4 us
    pallas_call x1, Pallas kernels, sort_atoms(): pl.pallas_call(sort_kernel, grid=(a_dev // block,), in_specs=[pl.BlockSpe...  18.7 us
    pallas_call x1, Pallas kernels, update_rows(): pl.pallas_call(update_kernel, grid=(a_dev // block,), in_specs=[pl.BlockS...  16.7 us
  transfers between devices with their start and end apart: 14, of which 14 were waited for; matrix products, arithmetic and copies ran while one was open for 1% of the time, Pallas kernels for 0%

commit v1 on v0

--- a/solution.py
+++ b/solution.py
@@ -46,9 +46,9 @@
     return (1.0 - s * s).astype(BF16), (s * c).astype(BF16)
 
 
-def sort_kernel(ids_ref, coords_ref, feat_ref, feat_out, coords_out):
+def sort_kernel(first, ids_ref, coords_ref, feat_ref, feat_out, coords_out):
     rows = feat_out.shape[0]
-    slots = pl.program_id(0) * rows + lax.broadcasted_iota(jnp.int32, (rows, 1), 0)
+    slots = first + pl.program_id(0) * rows + lax.broadcasted_iota(jnp.int32, (rows, 1), 0)
     pick = jnp.where(slots == ids_ref[...], 1.0, 0.0).astype(BF16)
     feat_out[...] = jnp.dot(pick, feat_ref[...], preferred_element_type=F32).astype(BF16)
     x = coords_ref[...]
@@ -61,13 +61,12 @@
     coords_out[...] = moved[0:8] + moved[8:16] + moved[16:24]
 
 
-def sort_atoms(slot_ids, coords, feat):
+def sort_atoms(places, padded, feat, first, count):
     a_dev, chans = feat.shape
-    block = min(512, a_dev)
-    padded = jnp.concatenate([coords, jnp.zeros((8 - coords.shape[0], a_dev), F32)], axis=0)
+    block = min(512, count)
     return pl.pallas_call(
-        sort_kernel,
-        grid=(a_dev // block,),
+        functools.partial(sort_kernel, first),
+        grid=(count // block,),
         in_specs=[
             pl.BlockSpec((1, a_dev), lambda i: (0, 0)),
             pl.BlockSpec((8, a_dev), lambda i: (0, 0)),
@@ -78,17 +77,20 @@
             pl.BlockSpec((8, block), lambda i: (0, i)),
         ],
         out_shape=[
-            jax.ShapeDtypeStruct((a_dev, chans), BF16),
-            jax.ShapeDtypeStruct((8, a_dev), F32),
+            jax.ShapeDtypeStruct((count, chans), BF16),
+            jax.ShapeDtypeStruct((8, count), F32),
         ],
         compiler_params=pltpu.CompilerParams(vmem_limit_bytes=48 * 1024 * 1024),
+        cost_estimate=pl.CostEstimate(
+            flops=4 * count * a_dev * chans, bytes_accessed=4 * count * chans, transcendentals=0
+        ),
         name="sort_atoms",
-    )(slot_ids, padded, feat)
-
-
-def waves_kernel(chunk, k_ref, x_ref, feat_ref, cos_ref, sin_ref, sums_ref):
-    rows, atoms = cos_ref.shape
-    sums_ref[...] = jnp.zeros_like(sums_ref)
+    )(places, padded, feat)
+
+
+def sums_kernel(chunk, k_ref, x_ref, feat_ref, sums_ref, totals):
+    rows, atoms = k_ref.shape[0], x_ref.shape[1]
+    totals[...] = jnp.zeros_like(totals)
     strip = 16
 
     def one_chunk(j, carry):
@@ -101,82 +103,115 @@
             c, s = cos_sin(turns)
             coses.append(c)
             sines.append(s)
-        c = jnp.concatenate(coses, axis=0)
-        s = jnp.concatenate(sines, axis=0)
-        cos_ref[:, lanes] = c
-        sin_ref[:, lanes] = s
         f = feat_ref[lanes, :]
-        sums_ref[0] += jnp.dot(c, f, preferred_element_type=F32)
-        sums_ref[1] += jnp.dot(s, f, preferred_element_type=F32)
+        totals[0] += jnp.dot(jnp.concatenate(coses, axis=0), f, preferred_element_type=F32)
+        totals[1] += jnp.dot(jnp.concatenate(sines, axis=0), f, preferred_element_type=F32)
         return carry
 
     lax.fori_loop(0, atoms // chunk, one_chunk, 0)
-
-
-def waves(k_turns, coords, feat):
+    sums_ref[...] = totals[...].astype(BF16)
+
+
+def wave_sums(k_turns, coords, feat):
     kspace = k_turns.shape[0]
     a_dev, chans = feat.shape
     block = min(256, kspace)
     return pl.pallas_call(
-        functools.partial(waves_kernel, min(512, a_dev)),
+        functools.partial(sums_kernel, min(512, a_dev)),
         grid=(kspace // block,),
         in_specs=[
             pl.BlockSpec((block, k_turns.shape[1]), lambda i: (i, 0)),
             pl.BlockSpec((8, a_dev), lambda i: (0, 0)),
             pl.BlockSpec((a_dev, chans), lambda i: (0, 0)),
         ],
-        out_specs=[
-            pl.BlockSpec((block, a_dev), lambda i: (i, 0)),
-            pl.BlockSpec((block, a_dev), lambda i: (i, 0)),
-            pl.BlockSpec((2, block, chans), lambda i: (0, i, 0)),
-        ],
-        out_shape=[
-            jax.ShapeDtypeStruct((kspace, a_dev), BF16),
-            jax.ShapeDtypeStruct((kspace, a_dev), BF16),
-            jax.ShapeDtypeStruct((2, kspace, chans), F32),
-        ],
+        out_specs=pl.BlockSpec((2, block, chans), lambda i: (0, i, 0)),
+        out_shape=jax.ShapeDtypeStruct((2, kspace, chans), BF16),
+        scratch_shapes=[pltpu.VMEM((2, block, chans), F32)],
         compiler_params=pltpu.CompilerParams(vmem_limit_bytes=48 * 1024 * 1024),
         cost_estimate=pl.CostEstimate(
-            flops=60 * kspace * a_dev + 4 * kspace * a_dev * chans,
-            bytes_accessed=4 * kspace * a_dev,
+            flops=10 * kspace * a_dev * chans, bytes_accessed=4 * kspace * chans, transcendentals=0
+        ),
+        name="wave_sums",
+    )(k_turns, coords, feat)
+
+
+def tables_kernel(chunk, k_ref, x_ref, cos_ref, sin_ref):
+    rows, atoms = cos_ref.shape
+    strip = 16
+
+    def one_chunk(j, carry):
+        lanes = pl.ds(pl.multiple_of(j * chunk, chunk), chunk)
+        x0, x1, x2 = x_ref[0:1, lanes], x_ref[1:2, lanes], x_ref[2:3, lanes]
+        for top in range(0, rows, strip):
+            k = k_ref[top : top + strip, :]
+            turns = k[:, 0:1] * x0 + k[:, 1:2] * x1 + k[:, 2:3] * x2
+            c, s = cos_sin(turns)
+            cos_ref[top : top + strip, lanes] = c
+            sin_ref[top : top + strip, lanes] = s
+        return carry
+
+    lax.fori_loop(0, atoms // chunk, one_chunk, 0)
+
+
+def wave_tables(k_turns, coords):
+    kspace = k_turns.shape[0]
+    atoms = coords.shape[1]
+    block = min(256, kspace)
+    return pl.pallas_call(
+        functools.partial(tables_kernel, min(512, atoms)),
+        grid=(kspace // block,),
+        in_specs=[
+            pl.BlockSpec((block, k_turns.shape[1]), lambda i: (i, 0)),
+            pl.BlockSpec((8, atoms), lambda i: (0, 0)),
+        ],
+        out_specs=[pl.BlockSpec((block, atoms), lambda i: (i, 0))] * 2,
+        out_shape=[jax.ShapeDtypeStruct((kspace, atoms), BF16)] * 2,
+        compiler_params=pltpu.CompilerParams(vmem_limit_bytes=48 * 1024 * 1024),
+        cost_estimate=pl.CostEstimate(
+            flops=2000 * kspace * atoms, bytes_accessed=4 * kspace * atoms, transcendentals=0
+        ),
+        name="wave_tables",
+    )(k_turns, coords)
+
+
+def update_kernel(parts, *refs):
+    filt_refs, refs = refs[:parts], refs[parts:]
+    table_refs, (out_ref, turned) = refs[: 2 * parts], refs[2 * parts :]
+    length = filt_refs[0].shape[1]
+
+    @pl.when(pl.program_id(0) == 0)
+    def _():
+        for n, filt_ref in enumerate(filt_refs):
+            for kind in range(2):
+                turned[2 * n + kind] = filt_ref[kind].astype(F32).T.astype(BF16)
+
+    total = jnp.dot(turned[0], table_refs[0][...], preferred_element_type=F32)
+    for n in range(1, 2 * parts):
+        total = total + jnp.dot(turned[n], table_refs[n][...], preferred_element_type=F32)
+    out_ref[...] = total.T.astype(BF16)
+
+
+def update_rows(filts, tables):
+    length, atoms = tables[0][0].shape
+    chans = filts[0].shape[2]
+    block = min(512, atoms)
+    flat = [table for pair in tables for table in pair]
+    return pl.pallas_call(
+        functools.partial(update_kernel, len(filts)),
+        grid=(atoms // block,),
+        in_specs=[pl.BlockSpec(filt.shape, lambda i: (0, 0, 0)) for filt in filts]
+        + [pl.BlockSpec((length, block), lambda i: (0, i)) for _ in flat],
+        out_specs=pl.BlockSpec((block, chans), lambda i: (i, 0)),
+        out_shape=jax.ShapeDtypeStruct((atoms, chans), BF16),
+        scratch_shapes=[pltpu.VMEM((len(flat), chans, length), BF16)],
+        compiler_params=pltpu.CompilerParams(vmem_limit_bytes=48 * 1024 * 1024),
+        cost_estimate=pl.CostEstimate(
+            flops=2 * len(flat) * length * atoms * chans,
+            bytes_accessed=2 * len(flat) * length * atoms,
             transcendentals=0,
         ),
-        name="waves",
-    )(k_turns, coords, feat)
-
-
-def update_kernel(filt_ref, cos_ref, sin_ref, out_ref, turned):
-    @pl.when(pl.program_id(0) == 0)
-    def _():
-        turned[0] = filt_ref[0].astype(F32).T.astype(BF16)
-        turned[1] = filt_ref[1].astype(F32).T.astype(BF16)
-
-    total = jnp.dot(turned[0], cos_ref[...], preferred_element_type=F32)
-    total = total + jnp.dot(turned[1], sin_ref[...], preferred_element_type=F32)
-    out_ref[...] = total.T.astype(BF16)
-
-
-def update_rows(filt, cosine, sine):
-    kspace, a_dev = cosine.shape
-    chans = filt.shape[2]
-    block = min(512, a_dev)
-    return pl.pallas_call(
-        update_kernel,
-        grid=(a_dev // block,),
-        in_specs=[
-            pl.BlockSpec((2, kspace, chans), lambda i: (0, 0, 0)),
-            pl.BlockSpec((kspace, block), lambda i: (0, i)),
-            pl.BlockSpec((kspace, block), lambda i: (0, i)),
-        ],
-        out_specs=pl.BlockSpec((block, chans), lambda i: (i, 0)),
-        out_shape=jax.ShapeDtypeStruct((a_dev, chans), BF16),
-        scratch_shapes=[pltpu.VMEM((2, chans, kspace), BF16)],
-        compiler_params=pltpu.CompilerParams(vmem_limit_bytes=48 * 1024 * 1024),
-        cost_estimate=pl.CostEstimate(
-            flops=4 * kspace * a_dev * chans, bytes_accessed=4 * kspace * a_dev, transcendentals=0
-        ),
         name="update_rows",
-    )(filt, cosine, sine)
+    )(*filts, *flat)
 
 
 def edges_kernel(src_ref, dst_ref, used_ref, table_ref, own_ref, send_ref, recv_ref, map_ref, out_ref, left, right, pair):
@@ -270,19 +305,15 @@
     return lax.ppermute(array, "atoms", pairs)
 
 
-def scatter_sum(array, dim):
+def sum_stage(array, dim, stride, size):
     devices = lax.axis_size("atoms")
-    me = lax.axis_index("atoms")
-    array = array.astype(BF16)
-    for stride, size in strides(devices):
-        place = (me // stride) % size
-        part = array.shape[dim] // size
-        total = lax.dynamic_slice_in_dim(array, place * part, part, dim).astype(F32)
-        for by in range(1, size):
-            away = lax.rem(place + by, size)
-            piece = lax.dynamic_slice_in_dim(array, away * part, part, dim)
-            total = total + shifted(piece, devices, stride, size, by).astype(F32)
-        array = total.astype(BF16)
+    place = (lax.axis_index("atoms") // stride) % size
+    part = array.shape[dim] // size
+    total = lax.dynamic_slice_in_dim(array, place * part, part, dim).astype(F32)
+    for by in range(1, size):
+        away = lax.rem(place + by, size)
+        piece = lax.dynamic_slice_in_dim(array, away * part, part, dim)
+        total = total + shifted(piece, devices, stride, size, by).astype(F32)
     return total
 
 
@@ -296,21 +327,34 @@
     return start
 
 
-def gather_parts(array, dim):
+def gather_stage(array, dim, stride, size):
     devices = lax.axis_size("atoms")
-    me = lax.axis_index("atoms")
-    for stride, size in reversed(strides(devices)):
-        place = (me // stride) % size
-        part = array.shape[dim]
-        shape = list(array.shape)
-        shape[dim] = part * size
-        whole = lax.dynamic_update_slice_in_dim(jnp.zeros(shape, array.dtype), array, place * part, dim)
-        for by in range(1, size):
-            came = lax.rem(place - by + size, size)
-            moved = shifted(array, devices, stride, size, by)
-            whole = lax.dynamic_update_slice_in_dim(whole, moved, came * part, dim)
-        array = whole
-    return array
+    place = (lax.axis_index("atoms") // stride) % size
+    part = array.shape[dim]
+    shape = list(array.shape)
+    shape[dim] = part * size
+    whole = lax.dynamic_update_slice_in_dim(jnp.zeros(shape, array.dtype), array, place * part, dim)
+    for by in range(1, size):
+        came = lax.rem(place - by + size, size)
+        moved = shifted(array, devices, stride, size, by)
+        whole = lax.dynamic_update_slice_in_dim(whole, moved, came * part, dim)
+    return whole
+
+
+def structure_stages(own_filter, norm_scale):
+    factors = strides(lax.axis_size("atoms"))
+    steps = []
+    for n, (stride, size) in enumerate(factors):
+        def add(array, stride=stride, size=size, last=n == len(factors) - 1):
+            total = sum_stage(array, 1, stride, size)
+            if last:
+                total = own_filter[None] * total * norm_scale
+            return total.astype(BF16)
+
+        steps.append(add)
+    for stride, size in reversed(factors):
+        steps.append(lambda array, stride=stride, size=size: gather_stage(array, 1, stride, size))
+    return steps
 
 
 def finish_rows(feat_rows, update, gain):
@@ -343,28 +387,103 @@
     kspace = kspace_vectors.shape[1]
     norm_scale = 1.0 / math.sqrt(a_dev * n_atoms * kspace * kspace_tally)
 
-    sorted_feat, sorted_coords = sort_atoms(spatial_home, particle_coordinates, particle_traits)
+    pieces = 2
+    padded = jnp.concatenate([particle_coordinates, jnp.zeros((8 - particle_coordinates.shape[0], a_dev), F32)], axis=0)
     k_turns = (kspace_vectors * (0.5 / math.pi)).T
-    cosine, sine, sums = waves(k_turns, sorted_coords, sorted_feat)
-    mine = scatter_sum(sums, 1)
-    own_filter = lax.dynamic_slice_in_dim(learned_kspace_filter, part_start(kspace), kspace // n_atoms, 0)
-    filt = (own_filter[None] * mine * norm_scale).astype(BF16)
-    filt = gather_parts(filt, 1)
-    partial = update_rows(filt, cosine, sine).reshape(n_atoms, group, chans)
-
+
+    share = sub_rows // pieces
+    count = a_dev // pieces
+    within = spatial_home % sub_rows
+    places = (within // share) * count + (spatial_home // sub_rows) * share + within % share
     kvec_index = lax.axis_index("kvec")
-    update_share = lax.dynamic_slice_in_dim(partial, kvec_index * sub_rows, sub_rows, 1).astype(F32)
-    for by in range(1, kspace_tally):
-        away = lax.rem(kvec_index + by, kspace_tally)
-        piece = lax.dynamic_slice_in_dim(partial, away * sub_rows, sub_rows, 1)
-        update_share = update_share + from_behind(piece, "kvec", by).astype(F32)
-    feat_share = lax.dynamic_slice_in_dim(
-        sorted_feat.reshape(n_atoms, group, chans), kvec_index * sub_rows, sub_rows, 1
-    )
-    node_share = finish_rows(feat_share, update_share, vertex_rescaling_gain)
-    arrived = lax.all_to_all(node_share, "atoms", split_axis=0, concat_axis=0, tiled=True)
-    gathered = lax.all_gather(arrived, "kvec", axis=1, tiled=True)
-    partition_rows = gathered.reshape(a_dev, chans)
+
+    k_part = kspace // pieces
+    quarter = k_part // 2
+    made = {}
+
+    def sums_of(key, first):
+        def work(k, x, f):
+            made[key] = wave_sums(lax.slice_in_dim(k, first, first + quarter), x, f)
+            return made[key]
+
+        return work
+
+    def sort_of(n):
+        def work(k, x, f):
+            made["sort", n] = sort_atoms(places, x, f, n * count, count)
+            return made["sort", n]
+
+        return work
+
+    def tables_of(n, half):
+        def work(k, x, f):
+            k_half = lax.slice_in_dim(k, half * k_part, (half + 1) * k_part)
+            made["tables", n, half] = wave_tables(k_half, made["sort", n][1])
+            return made["tables", n, half]
+
+        return work
+
+    works = [
+        sums_of("c", k_part),
+        sums_of("d", k_part + quarter),
+        sort_of(0),
+        tables_of(0, 0),
+        tables_of(0, 1),
+        sort_of(1),
+        tables_of(1, 0),
+        tables_of(1, 1),
+    ]
+    steps = []
+    for n in range(pieces):
+        own_filter = lax.dynamic_slice_in_dim(
+            learned_kspace_filter, n * k_part + part_start(k_part), k_part // n_atoms, 0
+        )
+        steps.append(structure_stages(own_filter, norm_scale))
+    lag = 2
+    inputs = (k_turns, padded, particle_traits)
+    states = [wave_sums(lax.slice_in_dim(k_turns, 0, k_part), padded, particle_traits), None]
+    for turn in range(max(len(works), lag + len(steps[1]))):
+        if turn == lag:
+            states[1] = jnp.concatenate([made["c"], made["d"]], axis=1)
+        states, inputs = lax.optimization_barrier((states, inputs))
+        done = works[turn](*inputs) if turn < len(works) else None
+        for n in range(pieces):
+            step = turn - n * lag
+            if 0 <= step < len(steps[n]):
+                states[n] = steps[n][step](states[n])
+        states, inputs, done = lax.optimization_barrier((states, inputs, done))
+        if turn < len(works):
+            made[list(made)[-1]] = done
+    filts = states
+
+    updates, feats = [], []
+    for n in range(pieces):
+        tables = [made["tables", n, half] for half in range(2)]
+        partial = update_rows(filts, tables).reshape(n_atoms, kspace_tally, share, chans)
+        update = [lax.dynamic_index_in_dim(partial, kvec_index, 1, False)]
+        for by in range(1, kspace_tally):
+            away = lax.rem(kvec_index + by, kspace_tally)
+            piece = lax.dynamic_index_in_dim(partial, away, 1, False)
+            update.append(from_behind(piece, "kvec", by))
+        updates.append(update)
+        feat = made["sort", n][0].reshape(n_atoms, kspace_tally, share, chans)
+        feats.append(lax.dynamic_index_in_dim(feat, kvec_index, 1, False))
+    partition_rows = jnp.zeros((n_atoms, kspace_tally, pieces, share, chans), BF16)
+    arrived = None
+    for n in range(pieces):
+        update = updates[n]
+        if n:
+            update, arrived = lax.optimization_barrier((update, arrived))
+        update = sum(term.astype(F32) for term in update)
+        node = finish_rows(feats[n], update, vertex_rescaling_gain)
+        arrived = lax.all_to_all(node, "atoms", split_axis=0, concat_axis=0, tiled=True)
+        for by in range(kspace_tally):
+            came = lax.rem(kvec_index - by + kspace_tally, kspace_tally)
+            moved = arrived if by == 0 else from_behind(arrived, "kvec", by)
+            partition_rows = lax.dynamic_update_slice(
+                partition_rows, moved[:, None, None], (0, came, n, 0, 0)
+            )
+    partition_rows = partition_rows.reshape(a_dev, chans)
     from_lower = from_behind(partition_rows[following_halo_lines[0]], "atoms", 1)
     from_upper = from_behind(partition_rows[previous_halo_lines[0]], "atoms", -1)
     row_table = jnp.concatenate([partition_rows, from_lower, from_upper], axis=0)

time: 305 us -> 281 us (0.921)
  waiting for transfers between devices: 114 us -> 59.8 us
  Pallas kernels: 106 us -> 143 us
  blocking collectives: 30.9 us -> 0 us
  starting transfers between devices: 10.9 us -> 40.2 us
  between operations: 15 us -> 2.19 us
  local copies, waits for them, and re-layouts: 14 us -> 24.8 us
  other arithmetic: 11.6 us -> 8.25 us
    ppermute x10 -> x20, waiting for transfers between devices: 50 us -> 4.9 us  [shifted(): return lax.ppermute(array, 'atoms', pairs)]
    pallas_call x3 -> x11, Pallas kernels: 80 us -> 116 us  [the longest x3 41.5 us: wave_sums(): pl.pallas_call(functools.partial(sums_kernel, min(512, a_dev)), grid=(ksp...]
    all_gather x1 -> x0, waiting for transfers between devices: 33.7 us -> none  [local(): gathered = lax.all_gather(arrived, 'kvec', axis=1, tiled=True)]
    all_to_all x1 -> x0, blocking collectives: 30.9 us -> none  [local(): lax.all_to_all(node_share, 'atoms', split_axis=0, concat_axis=0, tiled=True)]
    ppermute x10 -> x20, starting transfers between devices: 8.71 us -> 22.8 us  [shifted(): return lax.ppermute(array, 'atoms', pairs)]
    ppermute x3 -> x6, waiting for transfers between devices: 30.2 us -> 43.4 us  [from_behind(): lax.ppermute(array, axis, [(i, (i + by) % devices) for i in range(devices)])]
    all_to_all x0 -> x2, starting transfers between devices: none -> 12.8 us  [local(): lax.all_to_all(node, 'atoms', split_axis=0, concat_axis=0, tiled=True)]
    all_to_all x0 -> x2, waiting for transfers between devices: none -> 11.5 us  [local(): lax.all_to_all(node, 'atoms', split_axis=0, concat_axis=0, tiled=True)]
  transfers between devices with their start and end apart: 14 -> 28, of which waited for: 14 -> 10; matrix products, arithmetic and copies ran while one was open for 1% -> 3% of each run, Pallas kernels for 0% -> 28%
where the time goes in v1:
time: 281 us; the launch traced here: 278 us
  Pallas kernels  143 us (51%)
  waiting for transfers between devices  59.8 us (21%)
  starting transfers between devices  40.2 us (14%)
  local copies, waits for them, and re-layouts  24.8 us (9%)
  other arithmetic  8.25 us (3%)
    ppermute x6, waiting for transfers between devices, from_behind(): lax.ppermute(array, axis, [(i, (i + by) % devices) for i in range(devices)])  43.4 us
    pallas_call x3, Pallas kernels, wave_sums(): pl.pallas_call(functools.partial(sums_kernel, min(512, a_dev)), grid=(ksp...  41.5 us
    pallas_call x4, Pallas kernels, wave_tables(): pl.pallas_call(functools.partial(tables_kernel, min(512, atoms)), grid=(k...  37.6 us
    pallas_call x1, Pallas kernels, edges(): pl.pallas_call(edges_kernel, grid=(e_dev // block,), in_specs=[scalars, s...  26.4 us
    ppermute x20, starting transfers between devices, shifted(): return lax.ppermute(array, 'atoms', pairs)  22.8 us
    pallas_call x2, Pallas kernels, sort_atoms(): pl.pallas_call(functools.partial(sort_kernel, first), grid=(count // bloc...  18.7 us
    pallas_call x2, Pallas kernels, update_rows(): pl.pallas_call(functools.partial(update_kernel, len(filts)), grid=(atoms...  18.4 us
    all_to_all x2, starting transfers between devices, local(): lax.all_to_all(node, 'atoms', split_axis=0, concat_axis=0, tiled=True)  12.8 us
  transfers between devices with their start and end apart: 28, of which 10 were waited for; matrix products, arithmetic and copies ran while one was open for 3% of the time, Pallas kernels for 28%

profile of v1, /device:TPU:23, one launch (start us, length us, event | category | flops | bytes accessed | tf_op | source)
XLA Modules:
  0.0 277.7 jit_solution(17992469271167896102)
XLA Ops:
  3.0 20.7 %wave_sums.3 = bf16[2,1024,256]{2,1,0:T(8,128)(2,1)S(1)} custom-call(f32[1024,3]{1,0:T(8,128)S(1)} %slice.32.k_ref, f32[8,4096]{1,0:T(8,128)S(1)} %concatenate.9.x_ref.coords_ref, bf16[4096,256]{1,0:T(8,128)(2,1)S(1)} %copy-done.13), custom_call_target="tpu_custom_call" | custom-call | flops 10737418240 | bytes 1048576 | tf_op jit(solution)/shard_map/wave_sums/pallas_call | solution.py:119
  28.0 10.4 %wave_sums.4 = bf16[2,512,256]{2,1,0:T(8,128)(2,1)S(1)} custom-call(f32[512,3]{1,0:T(8,128)S(1)} %slice.22.k_ref, f32[8,4096]{1,0:T(8,128)S(1)} %concatenate.9.x_ref.coords_ref, bf16[4096,256]{1,0:T(8,128)(2,1)S(1)} %copy-done.13), custom_call_target="tpu_custom_call" | custom-call | flops 5368709120 | bytes 524288 | tf_op jit(solution)/shard_map/wave_sums/pallas_call | solution.py:119
  40.0 10.4 %wave_sums.5 = bf16[2,512,256]{2,1,0:T(8,128)(2,1)S(1)} custom-call(f32[512,3]{1,0:T(8,128)S(1)} %slice.23.k_ref, f32[8,4096]{1,0:T(8,128)S(1)} %concatenate.9.x_ref.coords_ref, bf16[4096,256]{1,0:T(8,128)(2,1)S(1)} %copy-done.13), custom_call_target="tpu_custom_call" | custom-call | flops 5368709120 | bytes 524288 | tf_op jit(solution)/shard_map/wave_sums/pallas_call | solution.py:119
  53.6 9.3 %sort_atoms.2 = (bf16[2048,256]{1,0:T(8,128)(2,1)S(1)}, f32[8,2048]{1,0:T(8,128)S(1)}) custom-call(s32[1,4096]{1,0:T(1,128)S(1)} %fusion.ids_ref, f32[8,4096]{1,0:T(8,128)S(1)} %concatenate.9.x_ref.coords_ref, bf16[4096,256]{1,0:T(8,128)(2,1)S(1)} %copy-done.13), custom_call_target="tpu_custom_call" | custom-call | flops 8589934592 | bytes 2097152 | tf_op jit(solution)/shard_map/sort_atoms/pallas_call | solution.py:67
  63.5 2.3 collective-permute-start.7
  65.8 2.0 collective-permute-start.8
  69.2 9.4 %wave_tables.4 = (bf16[1024,2048]{1,0:T(8,128)(2,1)S(1)}, bf16[1024,2048]{1,0:T(8,128)(2,1)}) custom-call(f32[1024,3]{1,0:T(8,128)S(1)} %slice.24.k_ref, f32[8,2048]{1,0:T(8,128)S(1)} %get-tuple-element.131.x_ref), custom_call_target="tpu_custom_call" | custom-call | flops 4194304000 | bytes 8388608 | tf_op jit(solution)/shard_map/wave_tables/pallas_call | solution.py:160
  78.5 2.0 copy-done.1
  80.8 9.5 %wave_tables.5 = (bf16[1024,2048]{1,0:T(8,128)(2,1)S(1)}, bf16[1024,2048]{1,0:T(8,128)(2,1)}) custom-call(f32[1024,3]{1,0:T(8,128)S(1)} %slice.25.k_ref, f32[8,2048]{1,0:T(8,128)S(1)} %get-tuple-element.131.x_ref), custom_call_target="tpu_custom_call" | custom-call | flops 4194304000 | bytes 8388608 | tf_op jit(solution)/shard_map/wave_tables/pallas_call | solution.py:160
  90.3 1.9 copy-done.2
  93.5 2.1 collective-permute-start.13
  97.8 3.0 %collective-permute-done.10 = bf16[2,256,256]{2,1,0:T(8,128)(2,1)S(1)} collective-permute-done((bf16[2,256,256]{2,1,0:T(8,128)(2,1)S(1)}, bf16[2,256,256]{2,1,0:T(8,128)(2,1)S(1)}, u32[]{:S(2)}, u32[]{:S(2)}) %collective-permute-start.10) | collective-permute-done | bytes 262176 | tf_op jit(solution)/shard_map/ppermute | solution.py:305
  102.4 2.3 collective-permute-start.17
  104.7 5.0 %collective-permute-start.14 = (bf16[2,512,256]{2,1,0:T(8,128)(2,1)S(1)}, bf16[2,512,256]{2,1,0:T(8,128)(2,1)S(1)}, u32[]{:S(2)}, u32[]{:S(2)}) collective-permute-start(bf16[2,512,256]{2,1,0:T(8,128)(2,1)S(1)} %constant_dynamic-update-slice_fusion.10), channel_id=1, source_target_pairs={{0,2},{2,0},{4,6},{6,4},{8,10},{10,8},{12,14},{14,12},{16,18},{18,... | collective-permute-start | bytes 1572872 | tf_op jit(solution)/shard_map/ppermute | solution.py:305
  109.7 9.3 %sort_atoms.3 = (bf16[2048,256]{1,0:T(8,128)(2,1)S(1)}, f32[8,2048]{1,0:T(8,128)S(1)}) custom-call(s32[1,4096]{1,0:T(1,128)S(1)} %fusion.ids_ref, f32[8,4096]{1,0:T(8,128)S(1)} %concatenate.9.x_ref.coords_ref, bf16[4096,256]{1,0:T(8,128)(2,1)S(1)} %copy-done.13), custom_call_target="tpu_custom_call" | custom-call | flops 8589934592 | bytes 2097152 | tf_op jit(solution)/shard_map/sort_atoms/pallas_call | solution.py:67
  121.8 9.4 %wave_tables.6 = (bf16[1024,2048]{1,0:T(8,128)(2,1)S(1)}, bf16[1024,2048]{1,0:T(8,128)(2,1)}) custom-call(f32[1024,3]{1,0:T(8,128)S(1)} %slice.26.k_ref, f32[8,2048]{1,0:T(8,128)S(1)} %get-tuple-element.164.x_ref), custom_call_target="tpu_custom_call" | custom-call | flops 4194304000 | bytes 8388608 | tf_op jit(solution)/shard_map/wave_tables/pallas_call | solution.py:160
  131.2 2.0 copy-done.3
  135.4 9.5 %wave_tables.7 = (bf16[1024,2048]{1,0:T(8,128)(2,1)S(1)}, bf16[1024,2048]{1,0:T(8,128)(2,1)}) custom-call(f32[1024,3]{1,0:T(8,128)S(1)} %slice.27.k_ref, f32[8,2048]{1,0:T(8,128)S(1)} %copy-done.15), custom_call_target="tpu_custom_call" | custom-call | flops 4194304000 | bytes 8388608 | tf_op jit(solution)/shard_map/wave_tables/pallas_call | solution.py:160
  144.9 1.9 copy-done.4
  147.9 9.2 %update_rows.2 = bf16[2048,256]{1,0:T(8,128)(2,1)S(1)} custom-call(bf16[2,1024,256]{2,1,0:T(8,128)(2,1)S(1)} %constant_dynamic-update-slice_fusion.8.refs_0_, bf16[2,1024,256]{2,1,0:T(8,128)(2,1)S(1)} %constant_dynamic-update-slice_fusion.refs_1_, bf16[1024,2048]{1,0:T(8,128)(2,1)} %copy-done.1, bf16[1024,2048]{1,0:T(8,128)(2,1)} %get-tuple-element.178.refs_3_, ...), custom_call_target="tpu_custom_call" | custom-call | flops 4294967296 | bytes 16777216 | tf_op jit(solution)/shard_map/update_rows/pallas_call | solution.py:199
  158.3 13.4 %collective-permute-done.20 = bf16[16,64,256]{2,1,0:T(8,128)(2,1)} collective-permute-done((bf16[16,64,256]{2,1,0:T(8,128)(2,1)}, bf16[16,64,256]{2,1,0:T(8,128)(2,1)}, u32[]{:S(2)}, u32[]{:S(2)}) %collective-permute-start.20) | collective-permute-done | bytes 524320 | tf_op jit(solution)/shard_map/ppermute | solution.py:286
  174.3 6.0 %all-to-all-start = ((bf16[16,64,256]{2,1,0:T(8,128)(2,1)}), bf16[16,64,256]{2,1,0:T(8,128)(2,1)S(1)}, u32[]{:S(2)}, u32[]{:S(2)}) async-start(bf16[16,64,256]{2,1,0:T(8,128)(2,1)} %multiply_convert_fusion.1), calls=%async_computation | async-start | bytes 1048576 | tf_op jit(solution)/shard_map/all_to_all | solution.py:479
  180.3 9.2 %update_rows.3 = bf16[2048,256]{1,0:T(8,128)(2,1)S(1)} custom-call(bf16[2,1024,256]{2,1,0:T(8,128)(2,1)S(1)} %constant_dynamic-update-slice_fusion.8.refs_0_, bf16[2,1024,256]{2,1,0:T(8,128)(2,1)S(1)} %constant_dynamic-update-slice_fusion.refs_1_, bf16[1024,2048]{1,0:T(8,128)(2,1)} %copy-done.3, bf16[1024,2048]{1,0:T(8,128)(2,1)} %get-tuple-element.183.refs_3_, ...), custom_call_target="tpu_custom_call" | custom-call | flops 4294967296 | bytes 16777216 | tf_op jit(solution)/shard_map/update_rows/pallas_call | solution.py:199
  189.9 13.0 %collective-permute-done.22 = bf16[16,64,256]{2,1,0:T(8,128)(2,1)} collective-permute-done((bf16[16,64,256]{2,1,0:T(8,128)(2,1)S(1)}, bf16[16,64,256]{2,1,0:T(8,128)(2,1)}, u32[]{:S(2)}, u32[]{:S(2)}) %collective-permute-start.22) | collective-permute-done | bytes 524320 | tf_op jit(solution)/shard_map/ppermute | solution.py:286
  205.5 6.9 %all-to-all-start.1 = ((bf16[16,64,256]{2,1,0:T(8,128)(2,1)}), bf16[16,64,256]{2,1,0:T(8,128)(2,1)S(1)}, u32[]{:S(2)}, u32[]{:S(2)}) async-start(bf16[16,64,256]{2,1,0:T(8,128)(2,1)} %multiply_convert_fusion), calls=%async_computation.1 | async-start | bytes 1048576 | tf_op jit(solution)/shard_map/all_to_all | solution.py:479
  212.7 11.5 %all-to-all-done.1 = bf16[16,64,256]{2,1,0:T(8,128)(2,1)S(1)} async-done(((bf16[16,64,256]{2,1,0:T(8,128)(2,1)}), bf16[16,64,256]{2,1,0:T(8,128)(2,1)S(1)}, u32[]{:S(2)}, u32[]{:S(2)}) %all-to-all-start.1) | async-done | bytes 524320 | tf_op jit(solution)/shard_map/all_to_all | solution.py:479
  226.8 10.1 %collective-permute-done.23 = bf16[16,64,256]{2,1,0:T(8,128)(2,1)S(1)} collective-permute-done((bf16[16,64,256]{2,1,0:T(8,128)(2,1)S(1)}, bf16[16,64,256]{2,1,0:T(8,128)(2,1)S(1)}, u32[]{:S(2)}, u32[]{:S(2)}) %collective-permute-start.23) | collective-permute-done | bytes 524320 | tf_op jit(solution)/shard_map/ppermute | solution.py:286
  237.0 2.0 gather_fusion
  239.0 3.5 %collective-permute-start.24 = (bf16[512,256]{1,0:T(8,128)(2,1)S(1)}, bf16[512,256]{1,0:T(8,128)(2,1)S(1)}, u32[]{:S(2)}, u32[]{:S(2)}) collective-permute-start(bf16[512,256]{1,0:T(8,128)(2,1)S(1)} %gather_fusion), channel_id=1, source_target_pairs={{0,2},{2,4},{4,6},{6,8},{8,10},{10,12},{12,14},{14,16},{16,18},{18... | collective-permute-start | bytes 786440 | tf_op jit(solution)/shard_map/ppermute | solution.py:286
  242.4 1.9 gather_fusion.1
  245.7 5.4 %collective-permute-done.25 = bf16[512,256]{1,0:T(8,128)(2,1)S(1)} collective-permute-done((bf16[512,256]{1,0:T(8,128)(2,1)S(1)}, bf16[512,256]{1,0:T(8,128)(2,1)S(1)}, u32[]{:S(2)}, u32[]{:S(2)}) %collective-permute-start.25) | collective-permute-done | bytes 262176 | tf_op jit(solution)/shard_map/ppermute | solution.py:286
  251.4 26.4 %edges.1 = bf16[196,4096]{1,0:T(8,128)(2,1)} custom-call(s32[4096]{0:T(1024)S(1)} %copy-done.11, s32[4096]{0:T(1024)S(1)} %copy-done.12, s32[1]{0:T(128)S(6)} %copy.62.used_ref, bf16[5120,256]{1,0:T(8,128)(2,1)S(1)} %pad_maximum_fusion.table_ref, bf16[4096,256]{1,0:T(8,128)(2,1)S(1)} %bitcast.53, bf16[256,256]{1,0:T(8,128)(2,1)S(1)} %copy-done.8, ...), custom_call_target="tpu_custom_call" | custom-call | tf_op jit(solution)/shard_map/edges/pallas_call | solution.py:268
  (154 shorter events, 34.9 us)
Async XLA Ops:
  3.0 22.3 %copy-start.22 = (s32[1,4096]{1,0:T(1,128)S(1)}, s32[1,4096]{1,0:T(1,128)}, u32[]{:S(2)}) copy-start(s32[1,4096]{1,0:T(1,128)} %param.18) | copy-start | bytes 49156
  24.6 13.9 %collective-permute-start = (bf16[2,512,256]{2,1,0:T(8,128)(2,1)}, bf16[2,512,256]{2,1,0:T(8,128)(2,1)}, u32[]{:S(2)}, u32[]{:S(2)}) collective-permute-start(bf16[2,512,256]{2,1,0:T(8,128)(2,1)} %constant_dynamic-slice_fusion.10), channel_id=1, source_target_pairs={{0,2},{2,0},{4,6},{6,4},{8,10},{10,8},{12,14},{14,12},{16,18},{18,... | collective-permute-start | bytes 1572872 | tf_op jit(solution)/shard_map/ppermute | solution.py:305
  39.7 10.7 %collective-permute-start.1 = (bf16[2,256,256]{2,1,0:T(8,128)(2,1)S(1)}, bf16[2,256,256]{2,1,0:T(8,128)(2,1)S(1)}, u32[]{:S(2)}, u32[]{:S(2)}) collective-permute-start(bf16[2,256,256]{2,1,0:T(8,128)(2,1)S(1)} %constant_dynamic-slice_fusion.9), channel_id=1, source_target_pairs={{0,4},{2,6},{4,0},{6,2},{8,12},{10,14},{12,8},{14,10},{16,20},{18,... | collective-permute-start | bytes 786440 | tf_op jit(solution)/shard_map/ppermute | solution.py:305
  50.6 12.4 %collective-permute-start.5 = (bf16[2,512,256]{2,1,0:T(8,128)(2,1)S(1)}, bf16[2,512,256]{2,1,0:T(8,128)(2,1)S(1)}, u32[]{:S(2)}, u32[]{:S(2)}) collective-permute-start(bf16[2,512,256]{2,1,0:T(8,128)(2,1)S(1)} %constant_dynamic-slice_fusion.5), channel_id=1, source_target_pairs={{0,2},{2,0},{4,6},{6,4},{8,10},{10,8},{12,14},{14,12},{16,18},{18,... | collective-permute-start | bytes 1572872 | tf_op jit(solution)/shard_map/ppermute | solution.py:305
  50.9 12.0 %collective-permute-start.2 = (bf16[2,64,256]{2,1,0:T(8,128)(2,1)S(1)}, bf16[2,64,256]{2,1,0:T(8,128)(2,1)S(1)}, u32[]{:S(2)}, u32[]{:S(2)}) collective-permute-start(bf16[2,64,256]{2,1,0:T(8,128)(2,1)S(1)} %get-tuple-element.199), channel_id=1, source_target_pairs={{0,8},{2,10},{4,12},{6,14},{8,16},{10,18},{12,20},{14,22},{16,24},... | collective-permute-start | bytes 196616 | tf_op jit(solution)/shard_map/ppermute | solution.py:305
  52.3 10.6 %collective-permute-start.3 = (bf16[2,64,256]{2,1,0:T(8,128)(2,1)S(1)}, bf16[2,64,256]{2,1,0:T(8,128)(2,1)S(1)}, u32[]{:S(2)}, u32[]{:S(2)}) collective-permute-start(bf16[2,64,256]{2,1,0:T(8,128)(2,1)S(1)} %get-tuple-element.201), channel_id=1, source_target_pairs={{0,16},{2,18},{4,20},{6,22},{8,24},{10,26},{12,28},{14,30},{16,0},... | collective-permute-start | bytes 196616 | tf_op jit(solution)/shard_map/ppermute | solution.py:305
  52.4 10.6 %collective-permute-start.4 = (bf16[2,64,256]{2,1,0:T(8,128)(2,1)S(1)}, bf16[2,64,256]{2,1,0:T(8,128)(2,1)S(1)}, u32[]{:S(2)}, u32[]{:S(2)}) collective-permute-start(bf16[2,64,256]{2,1,0:T(8,128)(2,1)S(1)} %get-tuple-element.200), channel_id=1, source_target_pairs={{0,24},{2,26},{4,28},{6,30},{8,0},{10,2},{12,4},{14,6},{16,8},{18,... | collective-permute-start | bytes 196616 | tf_op jit(solution)/shard_map/ppermute | solution.py:305
  63.2 17.4 %collective-permute-start.6 = (bf16[2,64,256]{2,1,0:T(8,128)(2,1)S(1)}, bf16[2,64,256]{2,1,0:T(8,128)(2,1)S(1)}, u32[]{:S(2)}, u32[]{:S(2)}) collective-permute-start(bf16[2,64,256]{2,1,0:T(8,128)(2,1)S(1)} %multiply_convert_fusion.3), channel_id=1, source_target_pairs={{0,8},{2,10},{4,12},{6,14},{8,16},{10,18},{12,20},{14,22},{16,24},... | collective-permute-start | bytes 196616 | tf_op jit(solution)/shard_map/ppermute | solution.py:305
  63.5 17.1 %collective-permute-start.7 = (bf16[2,64,256]{2,1,0:T(8,128)(2,1)S(1)}, bf16[2,64,256]{2,1,0:T(8,128)(2,1)S(1)}, u32[]{:S(2)}, u32[]{:S(2)}) collective-permute-start(bf16[2,64,256]{2,1,0:T(8,128)(2,1)S(1)} %multiply_convert_fusion.3), channel_id=1, source_target_pairs={{0,16},{2,18},{4,20},{6,22},{8,24},{10,26},{12,28},{14,30},{16,0},... | collective-permute-start | bytes 196616 | tf_op jit(solution)/shard_map/ppermute | solution.py:305
  65.8 14.8 %collective-permute-start.8 = (bf16[2,64,256]{2,1,0:T(8,128)(2,1)S(1)}, bf16[2,64,256]{2,1,0:T(8,128)(2,1)S(1)}, u32[]{:S(2)}, u32[]{:S(2)}) collective-permute-start(bf16[2,64,256]{2,1,0:T(8,128)(2,1)S(1)} %multiply_convert_fusion.3), channel_id=1, source_target_pairs={{0,24},{2,26},{4,28},{6,30},{8,0},{10,2},{12,4},{14,6},{16,8},{18,... | collective-permute-start | bytes 196616 | tf_op jit(solution)/shard_map/ppermute | solution.py:305
  67.8 12.8 %collective-permute-start.9 = (bf16[2,256,256]{2,1,0:T(8,128)(2,1)S(1)}, bf16[2,256,256]{2,1,0:T(8,128)(2,1)S(1)}, u32[]{:S(2)}, u32[]{:S(2)}) collective-permute-start(bf16[2,256,256]{2,1,0:T(8,128)(2,1)S(1)} %constant_dynamic-slice_fusion.4), channel_id=1, source_target_pairs={{0,4},{2,6},{4,0},{6,2},{8,12},{10,14},{12,8},{14,10},{16,20},{18,... | collective-permute-start | bytes 786440 | tf_op jit(solution)/shard_map/ppermute | solution.py:305
  80.8 17.0 %copy-start.19 = (f32[64,256]{1,0:T(8,128)S(1)}, f32[64,256]{1,0:T(8,128)}, u32[]{:S(2)}) copy-start(f32[64,256]{1,0:T(8,128)} %get-tuple-element.192) | copy-start | bytes 196612
  92.2 3.6 %collective-permute-start.11 = (bf16[2,64,256]{2,1,0:T(8,128)(2,1)S(1)}, bf16[2,64,256]{2,1,0:T(8,128)(2,1)S(1)}, u32[]{:S(2)}, u32[]{:S(2)}) collective-permute-start(bf16[2,64,256]{2,1,0:T(8,128)(2,1)S(1)} %get-tuple-element.196), channel_id=1, source_target_pairs={{0,8},{2,10},{4,12},{6,14},{8,16},{10,18},{12,20},{14,22},{16,24},... | collective-permute-start | bytes 196616 | tf_op jit(solution)/shard_map/ppermute | solution.py:305
  92.3 4.1 %collective-permute-start.12 = (bf16[2,64,256]{2,1,0:T(8,128)(2,1)S(1)}, bf16[2,64,256]{2,1,0:T(8,128)(2,1)S(1)}, u32[]{:S(2)}, u32[]{:S(2)}) collective-permute-start(bf16[2,64,256]{2,1,0:T(8,128)(2,1)S(1)} %get-tuple-element.198), channel_id=1, source_target_pairs={{0,16},{2,18},{4,20},{6,22},{8,24},{10,26},{12,28},{14,30},{16,0},... | collective-permute-start | bytes 196616 | tf_op jit(solution)/shard_map/ppermute | solution.py:305
  93.5 4.3 %collective-permute-start.13 = (bf16[2,64,256]{2,1,0:T(8,128)(2,1)S(1)}, bf16[2,64,256]{2,1,0:T(8,128)(2,1)S(1)}, u32[]{:S(2)}, u32[]{:S(2)}) collective-permute-start(bf16[2,64,256]{2,1,0:T(8,128)(2,1)S(1)} %get-tuple-element.197), channel_id=1, source_target_pairs={{0,24},{2,26},{4,28},{6,30},{8,0},{10,2},{12,4},{14,6},{16,8},{18,... | collective-permute-start | bytes 196616 | tf_op jit(solution)/shard_map/ppermute | solution.py:305
  95.5 5.2 %collective-permute-start.10 = (bf16[2,256,256]{2,1,0:T(8,128)(2,1)S(1)}, bf16[2,256,256]{2,1,0:T(8,128)(2,1)S(1)}, u32[]{:S(2)}, u32[]{:S(2)}) collective-permute-start(bf16[2,256,256]{2,1,0:T(8,128)(2,1)S(1)} %constant_dynamic-update-slice_fusion.12), channel_id=1, source_target_pairs={{0,4},{2,6},{4,0},{6,2},{8,12},{10,14},{12,8},{14,10},{16,20},{18,... | collective-permute-start | bytes 786440 | tf_op jit(solution)/shard_map/ppermute | solution.py:305
  100.8 18.4 %collective-permute-start.15 = (bf16[2,64,256]{2,1,0:T(8,128)(2,1)S(1)}, bf16[2,64,256]{2,1,0:T(8,128)(2,1)S(1)}, u32[]{:S(2)}, u32[]{:S(2)}) collective-permute-start(bf16[2,64,256]{2,1,0:T(8,128)(2,1)S(1)} %multiply_convert_fusion.2), channel_id=1, source_target_pairs={{0,8},{2,10},{4,12},{6,14},{8,16},{10,18},{12,20},{14,22},{16,24},... | collective-permute-start | bytes 196616 | tf_op jit(solution)/shard_map/ppermute | solution.py:305
  100.9 18.4 %collective-permute-start.16 = (bf16[2,64,256]{2,1,0:T(8,128)(2,1)S(1)}, bf16[2,64,256]{2,1,0:T(8,128)(2,1)S(1)}, u32[]{:S(2)}, u32[]{:S(2)}) collective-permute-start(bf16[2,64,256]{2,1,0:T(8,128)(2,1)S(1)} %multiply_convert_fusion.2), channel_id=1, source_target_pairs={{0,16},{2,18},{4,20},{6,22},{8,24},{10,26},{12,28},{14,30},{16,0},... | collective-permute-start | bytes 196616 | tf_op jit(solution)/shard_map/ppermute | solution.py:305
  102.4 16.9 %collective-permute-start.17 = (bf16[2,64,256]{2,1,0:T(8,128)(2,1)S(1)}, bf16[2,64,256]{2,1,0:T(8,128)(2,1)S(1)}, u32[]{:S(2)}, u32[]{:S(2)}) collective-permute-start(bf16[2,64,256]{2,1,0:T(8,128)(2,1)S(1)} %multiply_convert_fusion.2), channel_id=1, source_target_pairs={{0,24},{2,26},{4,28},{6,30},{8,0},{10,2},{12,4},{14,6},{16,8},{18,... | collective-permute-start | bytes 196616 | tf_op jit(solution)/shard_map/ppermute | solution.py:305
  104.7 14.6 %collective-permute-start.14 = (bf16[2,512,256]{2,1,0:T(8,128)(2,1)S(1)}, bf16[2,512,256]{2,1,0:T(8,128)(2,1)S(1)}, u32[]{:S(2)}, u32[]{:S(2)}) collective-permute-start(bf16[2,512,256]{2,1,0:T(8,128)(2,1)S(1)} %constant_dynamic-update-slice_fusion.10), channel_id=1, source_target_pairs={{0,2},{2,0},{4,6},{6,4},{8,10},{10,8},{12,14},{14,12},{16,18},{18,... | collective-permute-start | bytes 1572872 | tf_op jit(solution)/shard_map/ppermute | solution.py:305
  120.0 13.2 %collective-permute-start.18 = (bf16[2,256,256]{2,1,0:T(8,128)(2,1)S(1)}, bf16[2,256,256]{2,1,0:T(8,128)(2,1)S(1)}, u32[]{:S(2)}, u32[]{:S(2)}) collective-permute-start(bf16[2,256,256]{2,1,0:T(8,128)(2,1)S(1)} %constant_dynamic-update-slice_fusion.4), channel_id=1, source_target_pairs={{0,4},{2,6},{4,0},{6,2},{8,12},{10,14},{12,8},{14,10},{16,20},{18,... | collective-permute-start | bytes 786440 | tf_op jit(solution)/shard_map/ppermute | solution.py:305
  133.9 12.9 %collective-permute-start.19 = (bf16[2,512,256]{2,1,0:T(8,128)(2,1)}, bf16[2,512,256]{2,1,0:T(8,128)(2,1)}, u32[]{:S(2)}, u32[]{:S(2)}) collective-permute-start(bf16[2,512,256]{2,1,0:T(8,128)(2,1)} %constant_dynamic-update-slice_fusion.2), channel_id=1, source_target_pairs={{0,2},{2,0},{4,6},{6,4},{8,10},{10,8},{12,14},{14,12},{16,18},{18,... | collective-permute-start | bytes 1572872 | tf_op jit(solution)/shard_map/ppermute | solution.py:305
  157.1 16.2 %copy-start.23 = (f32[256]{0:T(256)S(1)}, f32[256]{0:T(256)}, u32[]{:S(2)}) copy-start(f32[256]{0:T(256)} %param.24) | copy-start | bytes 3076
  158.0 13.6 %collective-permute-start.20 = (bf16[16,64,256]{2,1,0:T(8,128)(2,1)}, bf16[16,64,256]{2,1,0:T(8,128)(2,1)}, u32[]{:S(2)}, u32[]{:S(2)}) collective-permute-start(bf16[16,64,256]{2,1,0:T(8,128)(2,1)} %dynamic-slice_bitcast_fusion.2), channel_id=1, source_target_pairs={{0,1},{1,0},{2,3},{3,2},{4,5},{5,4},{6,7},{7,6},{8,9},{9,8},{10,11... | collective-permute-start | bytes 1572872 | tf_op jit(solution)/shard_map/ppermute | solution.py:286
  174.3 28.6 %all-to-all-start = ((bf16[16,64,256]{2,1,0:T(8,128)(2,1)}), bf16[16,64,256]{2,1,0:T(8,128)(2,1)S(1)}, u32[]{:S(2)}, u32[]{:S(2)}) async-start(bf16[16,64,256]{2,1,0:T(8,128)(2,1)} %multiply_convert_fusion.1), calls=%async_computation | async-start | bytes 1048576 | tf_op jit(solution)/shard_map/all_to_all | solution.py:479
  189.6 13.3 %collective-permute-start.22 = (bf16[16,64,256]{2,1,0:T(8,128)(2,1)S(1)}, bf16[16,64,256]{2,1,0:T(8,128)(2,1)}, u32[]{:S(2)}, u32[]{:S(2)}) collective-permute-start(bf16[16,64,256]{2,1,0:T(8,128)(2,1)S(1)} %get-tuple-element.194), channel_id=1, source_target_pairs={{0,1},{1,0},{2,3},{3,2},{4,5},{5,4},{6,7},{7,6},{8,9},{9,8},{10,11... | collective-permute-start | bytes 1572872 | tf_op jit(solution)/shard_map/ppermute | solution.py:286
  205.5 18.6 %all-to-all-start.1 = ((bf16[16,64,256]{2,1,0:T(8,128)(2,1)}), bf16[16,64,256]{2,1,0:T(8,128)(2,1)S(1)}, u32[]{:S(2)}, u32[]{:S(2)}) async-start(bf16[16,64,256]{2,1,0:T(8,128)(2,1)} %multiply_convert_fusion), calls=%async_computation.1 | async-start | bytes 1048576 | tf_op jit(solution)/shard_map/all_to_all | solution.py:479
  212.4 13.3 %collective-permute-start.21 = (bf16[16,64,256]{2,1,0:T(8,128)(2,1)S(1)}, bf16[16,64,256]{2,1,0:T(8,128)(2,1)}, u32[]{:S(2)}, u32[]{:S(2)}) collective-permute-start(bf16[16,64,256]{2,1,0:T(8,128)(2,1)S(1)} %all-to-all-done), channel_id=1, source_target_pairs={{0,1},{1,0},{2,3},{3,2},{4,5},{5,4},{6,7},{7,6},{8,9},{9,8},{10,11... | collective-permute-start | bytes 1572872 | tf_op jit(solution)/shard_map/ppermute | solution.py:286
  224.2 12.8 %collective-permute-start.23 = (bf16[16,64,256]{2,1,0:T(8,128)(2,1)S(1)}, bf16[16,64,256]{2,1,0:T(8,128)(2,1)S(1)}, u32[]{:S(2)}, u32[]{:S(2)}) collective-permute-start(bf16[16,64,256]{2,1,0:T(8,128)(2,1)S(1)} %all-to-all-done.1), channel_id=1, source_target_pairs={{0,1},{1,0},{2,3},{3,2},{4,5},{5,4},{6,7},{7,6},{8,9},{9,8},{10,11... | collective-permute-start | bytes 1572872 | tf_op jit(solution)/shard_map/ppermute | solution.py:286
  237.0 14.3 %copy-start = (bf16[16,2,2,64,256]{4,3,2,1,0:T(8,128)(2,1)}, bf16[16,2,2,64,256]{4,3,2,1,0:T(8,128)(2,1)S(1)}, u32[]{:S(2)}) copy-start(bf16[16,2,2,64,256]{4,3,2,1,0:T(8,128)(2,1)S(1)} %bitcast_dynamic-update-slice_fusion.3) | copy-start | bytes 6291460
  239.0 6.8 %collective-permute-start.24 = (bf16[512,256]{1,0:T(8,128)(2,1)S(1)}, bf16[512,256]{1,0:T(8,128)(2,1)S(1)}, u32[]{:S(2)}, u32[]{:S(2)}) collective-permute-start(bf16[512,256]{1,0:T(8,128)(2,1)S(1)} %gather_fusion), channel_id=1, source_target_pairs={{0,2},{2,4},{4,6},{6,8},{8,10},{10,12},{12,14},{14,16},{16,18},{18... | collective-permute-start | bytes 786440 | tf_op jit(solution)/shard_map/ppermute | solution.py:286
  244.4 6.7 %collective-permute-start.25 = (bf16[512,256]{1,0:T(8,128)(2,1)S(1)}, bf16[512,256]{1,0:T(8,128)(2,1)S(1)}, u32[]{:S(2)}, u32[]{:S(2)}) collective-permute-start(bf16[512,256]{1,0:T(8,128)(2,1)S(1)} %gather_fusion.1), channel_id=1, source_target_pairs={{0,30},{2,0},{4,2},{6,4},{8,6},{10,8},{12,10},{14,12},{16,14},{18,... | collective-permute-start | bytes 786440 | tf_op jit(solution)/shard_map/ppermute | solution.py:286
  (22 other events, 123.0 us)

commit v2 on v1

--- a/solution.py
+++ b/solution.py
@@ -88,7 +88,7 @@
     )(places, padded, feat)
 
 
-def sums_kernel(chunk, k_ref, x_ref, feat_ref, sums_ref, totals):
+def sums_kernel(chunk, k_ref, x_ref, feat_ref, sums_ref, cos_ref, sin_ref, totals):
     rows, atoms = k_ref.shape[0], x_ref.shape[1]
     totals[...] = jnp.zeros_like(totals)
     strip = 16
@@ -103,9 +103,13 @@
             c, s = cos_sin(turns)
             coses.append(c)
             sines.append(s)
+        c = jnp.concatenate(coses, axis=0)
+        s = jnp.concatenate(sines, axis=0)
+        cos_ref[:, lanes] = c
+        sin_ref[:, lanes] = s
         f = feat_ref[lanes, :]
-        totals[0] += jnp.dot(jnp.concatenate(coses, axis=0), f, preferred_element_type=F32)
-        totals[1] += jnp.dot(jnp.concatenate(sines, axis=0), f, preferred_element_type=F32)
+        totals[0] += jnp.dot(c, f, preferred_element_type=F32)
+        totals[1] += jnp.dot(s, f, preferred_element_type=F32)
         return carry
 
     lax.fori_loop(0, atoms // chunk, one_chunk, 0)
@@ -124,8 +128,10 @@
             pl.BlockSpec((8, a_dev), lambda i: (0, 0)),
             pl.BlockSpec((a_dev, chans), lambda i: (0, 0)),
         ],
-        out_specs=pl.BlockSpec((2, block, chans), lambda i: (0, i, 0)),
-        out_shape=jax.ShapeDtypeStruct((2, kspace, chans), BF16),
+        out_specs=[pl.BlockSpec((2, block, chans), lambda i: (0, i, 0))]
+        + [pl.BlockSpec((block, a_dev), lambda i: (i, 0))] * 2,
+        out_shape=[jax.ShapeDtypeStruct((2, kspace, chans), BF16)]
+        + [jax.ShapeDtypeStruct((kspace, a_dev), BF16)] * 2,
         scratch_shapes=[pltpu.VMEM((2, block, chans), F32)],
         compiler_params=pltpu.CompilerParams(vmem_limit_bytes=48 * 1024 * 1024),
         cost_estimate=pl.CostEstimate(
@@ -133,45 +139,6 @@
         ),
         name="wave_sums",
     )(k_turns, coords, feat)
-
-
-def tables_kernel(chunk, k_ref, x_ref, cos_ref, sin_ref):
-    rows, atoms = cos_ref.shape
-    strip = 16
-
-    def one_chunk(j, carry):
-        lanes = pl.ds(pl.multiple_of(j * chunk, chunk), chunk)
-        x0, x1, x2 = x_ref[0:1, lanes], x_ref[1:2, lanes], x_ref[2:3, lanes]
-        for top in range(0, rows, strip):
-            k = k_ref[top : top + strip, :]
-            turns = k[:, 0:1] * x0 + k[:, 1:2] * x1 + k[:, 2:3] * x2
-            c, s = cos_sin(turns)
-            cos_ref[top : top + strip, lanes] = c
-            sin_ref[top : top + strip, lanes] = s
-        return carry
-
-    lax.fori_loop(0, atoms // chunk, one_chunk, 0)
-
-
-def wave_tables(k_turns, coords):
-    kspace = k_turns.shape[0]
-    atoms = coords.shape[1]
-    block = min(256, kspace)
-    return pl.pallas_call(
-        functools.partial(tables_kernel, min(512, atoms)),
-        grid=(kspace // block,),
-        in_specs=[
-            pl.BlockSpec((block, k_turns.shape[1]), lambda i: (i, 0)),
-            pl.BlockSpec((8, atoms), lambda i: (0, 0)),
-        ],
-        out_specs=[pl.BlockSpec((block, atoms), lambda i: (i, 0))] * 2,
-        out_shape=[jax.ShapeDtypeStruct((kspace, atoms), BF16)] * 2,
-        compiler_params=pltpu.CompilerParams(vmem_limit_bytes=48 * 1024 * 1024),
-        cost_estimate=pl.CostEstimate(
-            flops=2000 * kspace * atoms, bytes_accessed=4 * kspace * atoms, transcendentals=0
-        ),
-        name="wave_tables",
-    )(k_turns, coords)
 
 
 def update_kernel(parts, *refs):
@@ -398,76 +365,51 @@
     kvec_index = lax.axis_index("kvec")
 
     k_part = kspace // pieces
-    quarter = k_part // 2
     made = {}
 
-    def sums_of(key, first):
-        def work(k, x, f):
-            made[key] = wave_sums(lax.slice_in_dim(k, first, first + quarter), x, f)
-            return made[key]
-
-        return work
-
-    def sort_of(n):
-        def work(k, x, f):
-            made["sort", n] = sort_atoms(places, x, f, n * count, count)
-            return made["sort", n]
-
-        return work
-
-    def tables_of(n, half):
-        def work(k, x, f):
-            k_half = lax.slice_in_dim(k, half * k_part, (half + 1) * k_part)
-            made["tables", n, half] = wave_tables(k_half, made["sort", n][1])
-            return made["tables", n, half]
-
-        return work
-
-    works = [
-        sums_of("c", k_part),
-        sums_of("d", k_part + quarter),
-        sort_of(0),
-        tables_of(0, 0),
-        tables_of(0, 1),
-        sort_of(1),
-        tables_of(1, 0),
-        tables_of(1, 1),
-    ]
+    def waves_of(half, n, k):
+        k_half = lax.slice_in_dim(k, half * k_part, (half + 1) * k_part)
+        made[half, n] = wave_sums(k_half, placed[n][1], placed[n][0])
+
+    def sums_of(half):
+        return sum(made[half, n][0].astype(F32) for n in range(pieces)).astype(BF16)
+
+    placed = [sort_atoms(places, padded, particle_traits, n * count, count) for n in range(pieces)]
     steps = []
-    for n in range(pieces):
+    for half in range(2):
         own_filter = lax.dynamic_slice_in_dim(
-            learned_kspace_filter, n * k_part + part_start(k_part), k_part // n_atoms, 0
+            learned_kspace_filter, half * k_part + part_start(k_part), k_part // n_atoms, 0
         )
         steps.append(structure_stages(own_filter, norm_scale))
-    lag = 2
-    inputs = (k_turns, padded, particle_traits)
-    states = [wave_sums(lax.slice_in_dim(k_turns, 0, k_part), padded, particle_traits), None]
-    for turn in range(max(len(works), lag + len(steps[1]))):
-        if turn == lag:
-            states[1] = jnp.concatenate([made["c"], made["d"]], axis=1)
-        states, inputs = lax.optimization_barrier((states, inputs))
-        done = works[turn](*inputs) if turn < len(works) else None
-        for n in range(pieces):
-            step = turn - n * lag
-            if 0 <= step < len(steps[n]):
-                states[n] = steps[n][step](states[n])
-        states, inputs, done = lax.optimization_barrier((states, inputs, done))
-        if turn < len(works):
-            made[list(made)[-1]] = done
-    filts = states
+    for n in range(pieces):
+        waves_of(0, n, k_turns)
+    state = sums_of(0)
+    for n in range(pieces):
+        state, k_turns = lax.optimization_barrier((state, k_turns))
+        waves_of(1, n, k_turns)
+        state = steps[0][n](state)
+        state, k_turns, made[1, n] = lax.optimization_barrier((state, k_turns, made[1, n]))
+    last = sums_of(1)
+    for turn in range(len(steps[1])):
+        last = steps[1][turn](last)
+        if turn + pieces < len(steps[0]):
+            state = steps[0][turn + pieces](state)
+    filts = [state, last]
 
     updates, feats = [], []
     for n in range(pieces):
-        tables = [made["tables", n, half] for half in range(2)]
-        partial = update_rows(filts, tables).reshape(n_atoms, kspace_tally, share, chans)
+        partial = update_rows(filts, [made[half, n][1:] for half in range(2)])
+        partial = partial.reshape(n_atoms, kspace_tally, share, chans)
         update = [lax.dynamic_index_in_dim(partial, kvec_index, 1, False)]
         for by in range(1, kspace_tally):
             away = lax.rem(kvec_index + by, kspace_tally)
             piece = lax.dynamic_index_in_dim(partial, away, 1, False)
             update.append(from_behind(piece, "kvec", by))
         updates.append(update)
-        feat = made["sort", n][0].reshape(n_atoms, kspace_tally, share, chans)
+        feat = placed[n][0].reshape(n_atoms, kspace_tally, share, chans)
         feats.append(lax.dynamic_index_in_dim(feat, kvec_index, 1, False))
+    for n in range(pieces - 1):
+        updates[n], updates[n + 1][0] = lax.optimization_barrier((updates[n], updates[n + 1][0]))
     partition_rows = jnp.zeros((n_atoms, kspace_tally, pieces, share, chans), BF16)
     arrived = None
     for n in range(pieces):

time: 281 us -> 243 us (0.86)
  Pallas kernels: 143 us -> 113 us
  local copies, waits for them, and re-layouts: 24.8 us -> 15.8 us
  starting transfers between devices: 40.2 us -> 43.3 us
    pallas_call x4 -> x0, Pallas kernels: 37.6 us -> none  [wave_tables(): pl.pallas_call(functools.partial(tables_kernel, min(512, atoms)), grid=(k...]
    ppermute x6, waiting for transfers between devices: 43.4 us -> 32.8 us  [from_behind(): lax.ppermute(array, axis, [(i, (i + by) % devices) for i in range(devices)])]
    ppermute x20, waiting for transfers between devices: 4.9 us -> 14.7 us  [shifted(): return lax.ppermute(array, 'atoms', pairs)]
    unnamed x52 -> x32, local copies, waits for them, and re-layouts: 9.55 us -> 1.67 us
    pallas_call x3 -> x4, Pallas kernels: 41.5 us -> 49 us  [wave_sums(): pl.pallas_call(functools.partial(sums_kernel, min(512, a_dev)), grid=(ksp...]
  transfers between devices with their start and end apart: 28 -> 28, of which waited for: 10 -> 17; matrix products, arithmetic and copies ran while one was open for 3% -> 4% of each run, Pallas kernels for 28% -> 14%
where the time goes in v2:
time: 243 us; the launch traced here: 241 us
  Pallas kernels  113 us (47%)
  waiting for transfers between devices  59 us (24%)
  starting transfers between devices  43.3 us (18%)
  local copies, waits for them, and re-layouts  15.8 us (7%)
  other arithmetic  8.33 us (3%)
    pallas_call x4, Pallas kernels, wave_sums(): pl.pallas_call(functools.partial(sums_kernel, min(512, a_dev)), grid=(ksp...  49 us
    ppermute x6, waiting for transfers between devices, from_behind(): lax.ppermute(array, axis, [(i, (i + by) % devices) for i in range(devices)])  32.8 us
    pallas_call x1, Pallas kernels, edges(): pl.pallas_call(edges_kernel, grid=(e_dev // block,), in_specs=[scalars, s...  26.4 us
    ppermute x20, starting transfers between devices, shifted(): return lax.ppermute(array, 'atoms', pairs)  24.4 us
    pallas_call x2, Pallas kernels, sort_atoms(): pl.pallas_call(functools.partial(sort_kernel, first), grid=(count // bloc...  18.7 us
    pallas_call x2, Pallas kernels, update_rows(): pl.pallas_call(functools.partial(update_kernel, len(filts)), grid=(atoms...  18.4 us
    ppermute x20, waiting for transfers between devices, shifted(): return lax.ppermute(array, 'atoms', pairs)  14.7 us
    all_to_all x2, starting transfers between devices, local(): lax.all_to_all(node, 'atoms', split_axis=0, concat_axis=0, tiled=True)  14.2 us
  transfers between devices with their start and end apart: 28, of which 17 were waited for; matrix products, arithmetic and copies ran while one was open for 4% of the time, Pallas kernels for 14%

profile of v2, /device:TPU:23, one launch (start us, length us, event | category | flops | bytes accessed | tf_op | source)
XLA Modules:
  0.0 240.8 jit_solution(12839487579331456911)
XLA Ops:
  2.5 1.6 copy-done.6
  4.1 9.3 %sort_atoms.2 = (bf16[2048,256]{1,0:T(8,128)(2,1)S(1)}, f32[8,2048]{1,0:T(8,128)S(1)}) custom-call(s32[1,4096]{1,0:T(1,128)S(1)} %fusion.ids_ref, f32[8,4096]{1,0:T(8,128)S(1)} %concatenate.6.coords_ref, bf16[4096,256]{1,0:T(8,128)(2,1)S(1)} %copy-done.6), custom_call_target="tpu_custom_call" | custom-call | flops 8589934592 | bytes 2097152 | tf_op jit(solution)/shard_map/sort_atoms/pallas_call | solution.py:67
  13.4 9.3 %sort_atoms.3 = (bf16[2048,256]{1,0:T(8,128)(2,1)S(1)}, f32[8,2048]{1,0:T(8,128)S(1)}) custom-call(s32[1,4096]{1,0:T(1,128)S(1)} %fusion.ids_ref, f32[8,4096]{1,0:T(8,128)S(1)} %concatenate.6.coords_ref, bf16[4096,256]{1,0:T(8,128)(2,1)S(1)} %copy-done.6), custom_call_target="tpu_custom_call" | custom-call | flops 8589934592 | bytes 2097152 | tf_op jit(solution)/shard_map/sort_atoms/pallas_call | solution.py:67
  23.2 12.3 %wave_sums.4 = (bf16[2,1024,256]{2,1,0:T(8,128)(2,1)S(1)}, bf16[1024,2048]{1,0:T(8,128)(2,1)}, bf16[1024,2048]{1,0:T(8,128)(2,1)}) custom-call(f32[1024,3]{1,0:T(8,128)S(1)} %slice.17.k_ref, f32[8,2048]{1,0:T(8,128)S(1)} %get-tuple-element.37.x_ref, bf16[2048,256]{1,0:T(8,128)(2,1)S(1)} %get-tuple-element.36.feat_ref), custom_call_target="tpu_custom_call" | custom-call | flops 5368709120 | bytes 1048576 | tf_op jit(solution)/shard_map/wave_sums/pallas_call | solution.py:123
  35.5 12.2 %wave_sums.5 = (bf16[2,1024,256]{2,1,0:T(8,128)(2,1)S(1)}, bf16[1024,2048]{1,0:T(8,128)(2,1)}, bf16[1024,2048]{1,0:T(8,128)(2,1)}) custom-call(f32[1024,3]{1,0:T(8,128)S(1)} %slice.17.k_ref, f32[8,2048]{1,0:T(8,128)S(1)} %get-tuple-element.39.x_ref, bf16[2048,256]{1,0:T(8,128)(2,1)S(1)} %get-tuple-element.40.feat_ref), custom_call_target="tpu_custom_call" | custom-call | flops 5368709120 | bytes 1048576 | tf_op jit(solution)/shard_map/wave_sums/pallas_call | solution.py:123
  50.7 12.3 %wave_sums.6 = (bf16[2,1024,256]{2,1,0:T(8,128)(2,1)S(1)}, bf16[1024,2048]{1,0:T(8,128)(2,1)}, bf16[1024,2048]{1,0:T(8,128)(2,1)}) custom-call(f32[1024,3]{1,0:T(8,128)S(1)} %slice.11.k_ref, f32[8,2048]{1,0:T(8,128)S(1)} %get-tuple-element.37.x_ref, bf16[2048,256]{1,0:T(8,128)(2,1)S(1)} %get-tuple-element.36.feat_ref), custom_call_target="tpu_custom_call" | custom-call | flops 5368709120 | bytes 1048576 | tf_op jit(solution)/shard_map/wave_sums/pallas_call | solution.py:123
  64.6 12.3 %wave_sums.7 = (bf16[2,1024,256]{2,1,0:T(8,128)(2,1)S(1)}, bf16[1024,2048]{1,0:T(8,128)(2,1)}, bf16[1024,2048]{1,0:T(8,128)(2,1)}) custom-call(f32[1024,3]{1,0:T(8,128)S(1)} %slice.12.k_ref, f32[8,2048]{1,0:T(8,128)S(1)} %get-tuple-element.39.x_ref, bf16[2048,256]{1,0:T(8,128)(2,1)S(1)} %get-tuple-element.40.feat_ref), custom_call_target="tpu_custom_call" | custom-call | flops 5368709120 | bytes 1048576 | tf_op jit(solution)/shard_map/wave_sums/pallas_call | solution.py:123
  85.0 1.5 collective-permute-done.4
  86.6 2.1 collective-permute-start.5
  92.0 1.6 collective-permute-start.13
  93.6 2.2 collective-permute-start.14
  95.8 2.0 collective-permute-done.12
  98.0 2.9 %collective-permute-done.14 = bf16[2,64,256]{2,1,0:T(8,128)(2,1)S(1)} collective-permute-done((bf16[2,64,256]{2,1,0:T(8,128)(2,1)S(1)}, bf16[2,64,256]{2,1,0:T(8,128)(2,1)S(1)}, u32[]{:S(2)}, u32[]{:S(2)}) %collective-permute-start.14) | collective-permute-done | bytes 65568 | tf_op jit(solution)/shard_map/ppermute | solution.py:272
  103.3 2.4 %collective-permute-start.16 = (bf16[2,64,256]{2,1,0:T(8,128)(2,1)S(1)}, bf16[2,64,256]{2,1,0:T(8,128)(2,1)S(1)}, u32[]{:S(2)}, u32[]{:S(2)}) collective-permute-start(bf16[2,64,256]{2,1,0:T(8,128)(2,1)S(1)} %get-tuple-element.75), channel_id=1, source_target_pairs={{0,16},{2,18},{4,20},{6,22},{8,24},{10,26},{12,28},{14,30},{16,0},... | collective-permute-start | bytes 196616 | tf_op jit(solution)/shard_map/ppermute | solution.py:272
  106.4 1.4 collective-permute-done.16
  107.8 1.8 collective-permute-done.17
  112.2 3.9 %collective-permute-done.18 = bf16[2,256,256]{2,1,0:T(8,128)(2,1)S(1)} collective-permute-done((bf16[2,256,256]{2,1,0:T(8,128)(2,1)S(1)}, bf16[2,256,256]{2,1,0:T(8,128)(2,1)S(1)}, u32[]{:S(2)}, u32[]{:S(2)}) %collective-permute-start.18) | collective-permute-done | bytes 262176 | tf_op jit(solution)/shard_map/ppermute | solution.py:272
  116.1 2.4 collective-permute-start.19
  121.3 9.2 %update_rows.2 = bf16[2048,256]{1,0:T(8,128)(2,1)S(1)} custom-call(bf16[2,1024,256]{2,1,0:T(8,128)(2,1)S(1)} %constant_dynamic-update-slice_fusion.8.refs_0_, bf16[2,1024,256]{2,1,0:T(8,128)(2,1)S(1)} %constant_dynamic-update-slice_fusion.refs_1_, bf16[1024,2048]{1,0:T(8,128)(2,1)} %get-tuple-element.57.refs_2_, ...), custom_call_target="tpu_custom_call" | custom-call | flops 4294967296 | bytes 16777216 | tf_op jit(solution)/shard_map/update_rows/pallas_call | solution.py:166
  130.9 9.2 %update_rows.3 = bf16[2048,256]{1,0:T(8,128)(2,1)S(1)} custom-call(bf16[2,1024,256]{2,1,0:T(8,128)(2,1)S(1)} %constant_dynamic-update-slice_fusion.8.refs_0_, bf16[2,1024,256]{2,1,0:T(8,128)(2,1)S(1)} %constant_dynamic-update-slice_fusion.refs_1_, bf16[1024,2048]{1,0:T(8,128)(2,1)} %get-tuple-element.61.refs_2_, ...), custom_call_target="tpu_custom_call" | custom-call | flops 4294967296 | bytes 16777216 | tf_op jit(solution)/shard_map/update_rows/pallas_call | solution.py:166
  141.1 2.8 %collective-permute-done.20 = bf16[16,64,256]{2,1,0:T(8,128)(2,1)S(1)} collective-permute-done((bf16[16,64,256]{2,1,0:T(8,128)(2,1)S(1)}, bf16[16,64,256]{2,1,0:T(8,128)(2,1)S(1)}, u32[]{:S(2)}, u32[]{:S(2)}) %collective-permute-start.20) | collective-permute-done | bytes 524320 | tf_op jit(solution)/shard_map/ppermute | solution.py:253
  145.3 7.3 %all-to-all-start = ((bf16[16,64,256]{2,1,0:T(8,128)(2,1)}), bf16[16,64,256]{2,1,0:T(8,128)(2,1)S(1)}, u32[]{:S(2)}, u32[]{:S(2)}) async-start(bf16[16,64,256]{2,1,0:T(8,128)(2,1)} %multiply_convert_fusion.1), calls=%async_computation | async-start | bytes 1048576 | tf_op jit(solution)/shard_map/all_to_all | solution.py:421
  153.0 13.0 %collective-permute-done.22 = bf16[16,64,256]{2,1,0:T(8,128)(2,1)} collective-permute-done((bf16[16,64,256]{2,1,0:T(8,128)(2,1)S(1)}, bf16[16,64,256]{2,1,0:T(8,128)(2,1)}, u32[]{:S(2)}, u32[]{:S(2)}) %collective-permute-start.22) | collective-permute-done | bytes 524320 | tf_op jit(solution)/shard_map/ppermute | solution.py:253
  166.0 1.6 multiply_reduce_fusion
  168.6 6.9 %all-to-all-start.1 = ((bf16[16,64,256]{2,1,0:T(8,128)(2,1)}), bf16[16,64,256]{2,1,0:T(8,128)(2,1)S(1)}, u32[]{:S(2)}, u32[]{:S(2)}) async-start(bf16[16,64,256]{2,1,0:T(8,128)(2,1)} %multiply_convert_fusion), calls=%async_computation.1 | async-start | bytes 1048576 | tf_op jit(solution)/shard_map/all_to_all | solution.py:421
  175.8 11.5 %all-to-all-done.1 = bf16[16,64,256]{2,1,0:T(8,128)(2,1)S(1)} async-done(((bf16[16,64,256]{2,1,0:T(8,128)(2,1)}), bf16[16,64,256]{2,1,0:T(8,128)(2,1)S(1)}, u32[]{:S(2)}, u32[]{:S(2)}) %all-to-all-start.1) | async-done | bytes 524320 | tf_op jit(solution)/shard_map/all_to_all | solution.py:421
  189.8 10.1 %collective-permute-done.23 = bf16[16,64,256]{2,1,0:T(8,128)(2,1)S(1)} collective-permute-done((bf16[16,64,256]{2,1,0:T(8,128)(2,1)S(1)}, bf16[16,64,256]{2,1,0:T(8,128)(2,1)S(1)}, u32[]{:S(2)}, u32[]{:S(2)}) %collective-permute-start.23) | collective-permute-done | bytes 524320 | tf_op jit(solution)/shard_map/ppermute | solution.py:253
  200.0 2.0 gather_fusion
  202.0 3.5 %collective-permute-start.24 = (bf16[512,256]{1,0:T(8,128)(2,1)S(1)}, bf16[512,256]{1,0:T(8,128)(2,1)S(1)}, u32[]{:S(2)}, u32[]{:S(2)}) collective-permute-start(bf16[512,256]{1,0:T(8,128)(2,1)S(1)} %gather_fusion), channel_id=1, source_target_pairs={{0,2},{2,4},{4,6},{6,8},{8,10},{10,12},{12,14},{14,16},{16,18},{18... | collective-permute-start | bytes 786440 | tf_op jit(solution)/shard_map/ppermute | solution.py:253
  205.5 1.9 gather_fusion.1
  208.8 5.4 %collective-permute-done.25 = bf16[512,256]{1,0:T(8,128)(2,1)S(1)} collective-permute-done((bf16[512,256]{1,0:T(8,128)(2,1)S(1)}, bf16[512,256]{1,0:T(8,128)(2,1)S(1)}, u32[]{:S(2)}, u32[]{:S(2)}) %collective-permute-start.25) | collective-permute-done | bytes 262176 | tf_op jit(solution)/shard_map/ppermute | solution.py:253
  214.4 26.4 %edges.1 = bf16[196,4096]{1,0:T(8,128)(2,1)} custom-call(s32[4096]{0:T(1024)S(1)} %copy-done.4, s32[4096]{0:T(1024)S(1)} %copy-done.5, s32[1]{0:T(128)S(6)} %copy.58.used_ref, bf16[5120,256]{1,0:T(8,128)(2,1)S(1)} %pad_maximum_fusion.table_ref, bf16[4096,256]{1,0:T(8,128)(2,1)S(1)} %bitcast.49, bf16[256,256]{1,0:T(8,128)(2,1)S(1)} %copy-done.1, ...), custom_call_target="tpu_custom_call" | custom-call | tf_op jit(solution)/shard_map/edges/pallas_call | solution.py:235
  (126 shorter events, 34.6 us)
Async XLA Ops:
  23.2 12.3 %copy-start.7 = (f32[3,2048]{0,1:T(8,128)}, f32[3,2048]{0,1:T(8,128)S(1)}, u32[]{:S(2)}) copy-start(f32[3,2048]{0,1:T(8,128)S(1)} %copy.31) | copy-start | bytes 73732
  48.9 14.1 %collective-permute-start = (bf16[2,512,256]{2,1,0:T(8,128)(2,1)}, bf16[2,512,256]{2,1,0:T(8,128)(2,1)}, u32[]{:S(2)}, u32[]{:S(2)}) collective-permute-start(bf16[2,512,256]{2,1,0:T(8,128)(2,1)} %constant_dynamic-slice_fusion.10), channel_id=1, source_target_pairs={{0,2},{2,0},{4,6},{6,4},{8,10},{10,8},{12,14},{14,12},{16,18},{18,... | collective-permute-start | bytes 1572872 | tf_op jit(solution)/shard_map/ppermute | solution.py:272
  50.7 12.3 %copy-start.10 = (bf16[2,1024,256]{2,1,0:T(8,128)(2,1)S(1)}, bf16[2,1024,256]{2,1,0:T(8,128)(2,1)}, u32[]{:S(2)}) copy-start(bf16[2,1024,256]{2,1,0:T(8,128)(2,1)} %copy-done.9) | copy-start | bytes 3145732
  50.7 13.5 %copy-start.8 = (f32[3,2048]{0,1:T(8,128)S(1)}, f32[3,2048]{0,1:T(8,128)}, u32[]{:S(2)}) copy-start(f32[3,2048]{0,1:T(8,128)} %copy-done.7) | copy-start | bytes 73732
  64.3 12.5 %collective-permute-start.1 = (bf16[2,256,256]{2,1,0:T(8,128)(2,1)S(1)}, bf16[2,256,256]{2,1,0:T(8,128)(2,1)S(1)}, u32[]{:S(2)}, u32[]{:S(2)}) collective-permute-start(bf16[2,256,256]{2,1,0:T(8,128)(2,1)S(1)} %constant_dynamic-slice_fusion.9), channel_id=1, source_target_pairs={{0,4},{2,6},{4,0},{6,2},{8,12},{10,14},{12,8},{14,10},{16,20},{18,... | collective-permute-start | bytes 786440 | tf_op jit(solution)/shard_map/ppermute | solution.py:272
  78.0 4.0 %collective-permute-start.10 = (bf16[2,512,256]{2,1,0:T(8,128)(2,1)}, bf16[2,512,256]{2,1,0:T(8,128)(2,1)}, u32[]{:S(2)}, u32[]{:S(2)}) collective-permute-start(bf16[2,512,256]{2,1,0:T(8,128)(2,1)} %constant_dynamic-slice_fusion.4), channel_id=1, source_target_pairs={{0,2},{2,0},{4,6},{6,4},{8,10},{10,8},{12,14},{14,12},{16,18},{18,... | collective-permute-start | bytes 1572872 | tf_op jit(solution)/shard_map/ppermute | solution.py:272
  79.4 5.1 %collective-permute-start.2 = (bf16[2,64,256]{2,1,0:T(8,128)(2,1)S(1)}, bf16[2,64,256]{2,1,0:T(8,128)(2,1)S(1)}, u32[]{:S(2)}, u32[]{:S(2)}) collective-permute-start(bf16[2,64,256]{2,1,0:T(8,128)(2,1)S(1)} %get-tuple-element.87), channel_id=1, source_target_pairs={{0,8},{2,10},{4,12},{6,14},{8,16},{10,18},{12,20},{14,22},{16,24},... | collective-permute-start | bytes 196616 | tf_op jit(solution)/shard_map/ppermute | solution.py:272
  80.7 4.2 %collective-permute-start.3 = (bf16[2,64,256]{2,1,0:T(8,128)(2,1)S(1)}, bf16[2,64,256]{2,1,0:T(8,128)(2,1)S(1)}, u32[]{:S(2)}, u32[]{:S(2)}) collective-permute-start(bf16[2,64,256]{2,1,0:T(8,128)(2,1)S(1)} %get-tuple-element.89), channel_id=1, source_target_pairs={{0,16},{2,18},{4,20},{6,22},{8,24},{10,26},{12,28},{14,30},{16,0},... | collective-permute-start | bytes 196616 | tf_op jit(solution)/shard_map/ppermute | solution.py:272
  80.8 5.7 %collective-permute-start.4 = (bf16[2,64,256]{2,1,0:T(8,128)(2,1)S(1)}, bf16[2,64,256]{2,1,0:T(8,128)(2,1)S(1)}, u32[]{:S(2)}, u32[]{:S(2)}) collective-permute-start(bf16[2,64,256]{2,1,0:T(8,128)(2,1)S(1)} %get-tuple-element.88), channel_id=1, source_target_pairs={{0,24},{2,26},{4,28},{6,30},{8,0},{10,2},{12,4},{14,6},{16,8},{18,... | collective-permute-start | bytes 196616 | tf_op jit(solution)/shard_map/ppermute | solution.py:272
  83.2 7.7 %collective-permute-start.11 = (bf16[2,256,256]{2,1,0:T(8,128)(2,1)S(1)}, bf16[2,256,256]{2,1,0:T(8,128)(2,1)S(1)}, u32[]{:S(2)}, u32[]{:S(2)}) collective-permute-start(bf16[2,256,256]{2,1,0:T(8,128)(2,1)S(1)} %constant_dynamic-slice_fusion.3), channel_id=1, source_target_pairs={{0,4},{2,6},{4,0},{6,2},{8,12},{10,14},{12,8},{14,10},{16,20},{18,... | collective-permute-start | bytes 786440 | tf_op jit(solution)/shard_map/ppermute | solution.py:272
  86.6 4.3 %collective-permute-start.5 = (bf16[2,64,256]{2,1,0:T(8,128)(2,1)S(1)}, bf16[2,64,256]{2,1,0:T(8,128)(2,1)S(1)}, u32[]{:S(2)}, u32[]{:S(2)}) collective-permute-start(bf16[2,64,256]{2,1,0:T(8,128)(2,1)S(1)} %get-tuple-element.77), channel_id=1, source_target_pairs={{0,8},{2,10},{4,12},{6,14},{8,16},{10,18},{12,20},{14,22},{16,24},... | collective-permute-start | bytes 196616 | tf_op jit(solution)/shard_map/ppermute | solution.py:272
  88.7 7.1 %collective-permute-start.6 = (bf16[2,64,256]{2,1,0:T(8,128)(2,1)S(1)}, bf16[2,64,256]{2,1,0:T(8,128)(2,1)S(1)}, u32[]{:S(2)}, u32[]{:S(2)}) collective-permute-start(bf16[2,64,256]{2,1,0:T(8,128)(2,1)S(1)} %get-tuple-element.77), channel_id=1, source_target_pairs={{0,16},{2,18},{4,20},{6,22},{8,24},{10,26},{12,28},{14,30},{16,0},... | collective-permute-start | bytes 196616 | tf_op jit(solution)/shard_map/ppermute | solution.py:272
  90.0 11.9 %collective-permute-start.7 = (bf16[2,64,256]{2,1,0:T(8,128)(2,1)S(1)}, bf16[2,64,256]{2,1,0:T(8,128)(2,1)S(1)}, u32[]{:S(2)}, u32[]{:S(2)}) collective-permute-start(bf16[2,64,256]{2,1,0:T(8,128)(2,1)S(1)} %get-tuple-element.77), channel_id=1, source_target_pairs={{0,24},{2,26},{4,28},{6,30},{8,0},{10,2},{12,4},{14,6},{16,8},{18,... | collective-permute-start | bytes 196616 | tf_op jit(solution)/shard_map/ppermute | solution.py:272
  91.0 6.8 %collective-permute-start.12 = (bf16[2,64,256]{2,1,0:T(8,128)(2,1)S(1)}, bf16[2,64,256]{2,1,0:T(8,128)(2,1)S(1)}, u32[]{:S(2)}, u32[]{:S(2)}) collective-permute-start(bf16[2,64,256]{2,1,0:T(8,128)(2,1)S(1)} %get-tuple-element.84), channel_id=1, source_target_pairs={{0,8},{2,10},{4,12},{6,14},{8,16},{10,18},{12,20},{14,22},{16,24},... | collective-permute-start | bytes 196616 | tf_op jit(solution)/shard_map/ppermute | solution.py:272
  92.0 5.9 %collective-permute-start.13 = (bf16[2,64,256]{2,1,0:T(8,128)(2,1)S(1)}, bf16[2,64,256]{2,1,0:T(8,128)(2,1)S(1)}, u32[]{:S(2)}, u32[]{:S(2)}) collective-permute-start(bf16[2,64,256]{2,1,0:T(8,128)(2,1)S(1)} %get-tuple-element.86), channel_id=1, source_target_pairs={{0,16},{2,18},{4,20},{6,22},{8,24},{10,26},{12,28},{14,30},{16,0},... | collective-permute-start | bytes 196616 | tf_op jit(solution)/shard_map/ppermute | solution.py:272
  93.6 7.3 %collective-permute-start.14 = (bf16[2,64,256]{2,1,0:T(8,128)(2,1)S(1)}, bf16[2,64,256]{2,1,0:T(8,128)(2,1)S(1)}, u32[]{:S(2)}, u32[]{:S(2)}) collective-permute-start(bf16[2,64,256]{2,1,0:T(8,128)(2,1)S(1)} %get-tuple-element.85), channel_id=1, source_target_pairs={{0,24},{2,26},{4,28},{6,30},{8,0},{10,2},{12,4},{14,6},{16,8},{18,... | collective-permute-start | bytes 196616 | tf_op jit(solution)/shard_map/ppermute | solution.py:272
  101.0 5.4 %collective-permute-start.15 = (bf16[2,64,256]{2,1,0:T(8,128)(2,1)S(1)}, bf16[2,64,256]{2,1,0:T(8,128)(2,1)S(1)}, u32[]{:S(2)}, u32[]{:S(2)}) collective-permute-start(bf16[2,64,256]{2,1,0:T(8,128)(2,1)S(1)} %get-tuple-element.75), channel_id=1, source_target_pairs={{0,8},{2,10},{4,12},{6,14},{8,16},{10,18},{12,20},{14,22},{16,24},... | collective-permute-start | bytes 196616 | tf_op jit(solution)/shard_map/ppermute | solution.py:272
  102.0 9.1 %collective-permute-start.8 = (bf16[2,256,256]{2,1,0:T(8,128)(2,1)S(1)}, bf16[2,256,256]{2,1,0:T(8,128)(2,1)S(1)}, u32[]{:S(2)}, u32[]{:S(2)}) collective-permute-start(bf16[2,256,256]{2,1,0:T(8,128)(2,1)S(1)} %constant_dynamic-update-slice_fusion.12), channel_id=1, source_target_pairs={{0,4},{2,6},{4,0},{6,2},{8,12},{10,14},{12,8},{14,10},{16,20},{18,... | collective-permute-start | bytes 786440 | tf_op jit(solution)/shard_map/ppermute | solution.py:272
  103.3 4.5 %collective-permute-start.16 = (bf16[2,64,256]{2,1,0:T(8,128)(2,1)S(1)}, bf16[2,64,256]{2,1,0:T(8,128)(2,1)S(1)}, u32[]{:S(2)}, u32[]{:S(2)}) collective-permute-start(bf16[2,64,256]{2,1,0:T(8,128)(2,1)S(1)} %get-tuple-element.75), channel_id=1, source_target_pairs={{0,16},{2,18},{4,20},{6,22},{8,24},{10,26},{12,28},{14,30},{16,0},... | collective-permute-start | bytes 196616 | tf_op jit(solution)/shard_map/ppermute | solution.py:272
  105.7 3.9 %collective-permute-start.17 = (bf16[2,64,256]{2,1,0:T(8,128)(2,1)S(1)}, bf16[2,64,256]{2,1,0:T(8,128)(2,1)S(1)}, u32[]{:S(2)}, u32[]{:S(2)}) collective-permute-start(bf16[2,64,256]{2,1,0:T(8,128)(2,1)S(1)} %get-tuple-element.75), channel_id=1, source_target_pairs={{0,24},{2,26},{4,28},{6,30},{8,0},{10,2},{12,4},{14,6},{16,8},{18,... | collective-permute-start | bytes 196616 | tf_op jit(solution)/shard_map/ppermute | solution.py:272
  109.7 6.5 %collective-permute-start.18 = (bf16[2,256,256]{2,1,0:T(8,128)(2,1)S(1)}, bf16[2,256,256]{2,1,0:T(8,128)(2,1)S(1)}, u32[]{:S(2)}, u32[]{:S(2)}) collective-permute-start(bf16[2,256,256]{2,1,0:T(8,128)(2,1)S(1)} %constant_dynamic-update-slice_fusion.4), channel_id=1, source_target_pairs={{0,4},{2,6},{4,0},{6,2},{8,12},{10,14},{12,8},{14,10},{16,20},{18,... | collective-permute-start | bytes 786440 | tf_op jit(solution)/shard_map/ppermute | solution.py:272
  111.2 7.5 %collective-permute-start.9 = (bf16[2,512,256]{2,1,0:T(8,128)(2,1)S(1)}, bf16[2,512,256]{2,1,0:T(8,128)(2,1)}, u32[]{:S(2)}, u32[]{:S(2)}) collective-permute-start(bf16[2,512,256]{2,1,0:T(8,128)(2,1)S(1)} %constant_dynamic-update-slice_fusion.10), channel_id=1, source_target_pairs={{0,2},{2,0},{4,6},{6,4},{8,10},{10,8},{12,14},{14,12},{16,18},{18,... | collective-permute-start | bytes 1572872 | tf_op jit(solution)/shard_map/ppermute | solution.py:272
  116.1 4.1 %collective-permute-start.19 = (bf16[2,512,256]{2,1,0:T(8,128)(2,1)S(1)}, bf16[2,512,256]{2,1,0:T(8,128)(2,1)}, u32[]{:S(2)}, u32[]{:S(2)}) collective-permute-start(bf16[2,512,256]{2,1,0:T(8,128)(2,1)S(1)} %constant_dynamic-update-slice_fusion.2), channel_id=1, source_target_pairs={{0,2},{2,0},{4,6},{6,4},{8,10},{10,8},{12,14},{14,12},{16,18},{18,... | collective-permute-start | bytes 1572872 | tf_op jit(solution)/shard_map/ppermute | solution.py:272
  130.6 13.2 %collective-permute-start.20 = (bf16[16,64,256]{2,1,0:T(8,128)(2,1)S(1)}, bf16[16,64,256]{2,1,0:T(8,128)(2,1)S(1)}, u32[]{:S(2)}, u32[]{:S(2)}) collective-permute-start(bf16[16,64,256]{2,1,0:T(8,128)(2,1)S(1)} %get-tuple-element.82), channel_id=1, source_target_pairs={{0,1},{1,0},{2,3},{3,2},{4,5},{5,4},{6,7},{7,6},{8,9},{9,8},{10,11... | collective-permute-start | bytes 1572872 | tf_op jit(solution)/shard_map/ppermute | solution.py:253
  145.3 20.7 %all-to-all-start = ((bf16[16,64,256]{2,1,0:T(8,128)(2,1)}), bf16[16,64,256]{2,1,0:T(8,128)(2,1)S(1)}, u32[]{:S(2)}, u32[]{:S(2)}) async-start(bf16[16,64,256]{2,1,0:T(8,128)(2,1)} %multiply_convert_fusion.1), calls=%async_computation | async-start | bytes 1048576 | tf_op jit(solution)/shard_map/all_to_all | solution.py:421
  152.7 13.3 %collective-permute-start.22 = (bf16[16,64,256]{2,1,0:T(8,128)(2,1)S(1)}, bf16[16,64,256]{2,1,0:T(8,128)(2,1)}, u32[]{:S(2)}, u32[]{:S(2)}) collective-permute-start(bf16[16,64,256]{2,1,0:T(8,128)(2,1)S(1)} %copy-done.11), channel_id=1, source_target_pairs={{0,1},{1,0},{2,3},{3,2},{4,5},{5,4},{6,7},{7,6},{8,9},{9,8},{10,11... | collective-permute-start | bytes 1572872 | tf_op jit(solution)/shard_map/ppermute | solution.py:253
  168.6 18.6 %all-to-all-start.1 = ((bf16[16,64,256]{2,1,0:T(8,128)(2,1)}), bf16[16,64,256]{2,1,0:T(8,128)(2,1)S(1)}, u32[]{:S(2)}, u32[]{:S(2)}) async-start(bf16[16,64,256]{2,1,0:T(8,128)(2,1)} %multiply_convert_fusion), calls=%async_computation.1 | async-start | bytes 1048576 | tf_op jit(solution)/shard_map/all_to_all | solution.py:421
  175.4 13.3 %collective-permute-start.21 = (bf16[16,64,256]{2,1,0:T(8,128)(2,1)S(1)}, bf16[16,64,256]{2,1,0:T(8,128)(2,1)}, u32[]{:S(2)}, u32[]{:S(2)}) collective-permute-start(bf16[16,64,256]{2,1,0:T(8,128)(2,1)S(1)} %all-to-all-done), channel_id=1, source_target_pairs={{0,1},{1,0},{2,3},{3,2},{4,5},{5,4},{6,7},{7,6},{8,9},{9,8},{10,11... | collective-permute-start | bytes 1572872 | tf_op jit(solution)/shard_map/ppermute | solution.py:253
  187.2 12.8 %collective-permute-start.23 = (bf16[16,64,256]{2,1,0:T(8,128)(2,1)S(1)}, bf16[16,64,256]{2,1,0:T(8,128)(2,1)S(1)}, u32[]{:S(2)}, u32[]{:S(2)}) collective-permute-start(bf16[16,64,256]{2,1,0:T(8,128)(2,1)S(1)} %all-to-all-done.1), channel_id=1, source_target_pairs={{0,1},{1,0},{2,3},{3,2},{4,5},{5,4},{6,7},{7,6},{8,9},{9,8},{10,11... | collective-permute-start | bytes 1572872 | tf_op jit(solution)/shard_map/ppermute | solution.py:253
  200.0 14.3 %copy-start = (bf16[16,2,2,64,256]{4,3,2,1,0:T(8,128)(2,1)}, bf16[16,2,2,64,256]{4,3,2,1,0:T(8,128)(2,1)S(1)}, u32[]{:S(2)}) copy-start(bf16[16,2,2,64,256]{4,3,2,1,0:T(8,128)(2,1)S(1)} %bitcast_dynamic-update-slice_fusion.3) | copy-start | bytes 6291460
  202.0 6.8 %collective-permute-start.24 = (bf16[512,256]{1,0:T(8,128)(2,1)S(1)}, bf16[512,256]{1,0:T(8,128)(2,1)S(1)}, u32[]{:S(2)}, u32[]{:S(2)}) collective-permute-start(bf16[512,256]{1,0:T(8,128)(2,1)S(1)} %gather_fusion), channel_id=1, source_target_pairs={{0,2},{2,4},{4,6},{6,8},{8,10},{10,12},{12,14},{14,16},{16,18},{18... | collective-permute-start | bytes 786440 | tf_op jit(solution)/shard_map/ppermute | solution.py:253
  207.4 6.7 %collective-permute-start.25 = (bf16[512,256]{1,0:T(8,128)(2,1)S(1)}, bf16[512,256]{1,0:T(8,128)(2,1)S(1)}, u32[]{:S(2)}, u32[]{:S(2)}) collective-permute-start(bf16[512,256]{1,0:T(8,128)(2,1)S(1)} %gather_fusion.1), channel_id=1, source_target_pairs={{0,30},{2,0},{4,2},{6,4},{8,6},{10,8},{12,10},{14,12},{16,14},{18,... | collective-permute-start | bytes 786440 | tf_op jit(solution)/shard_map/ppermute | solution.py:253
  (12 other events, 75.6 us)

commit v3 on v2

--- a/solution.py
+++ b/solution.py
@@ -354,7 +354,7 @@
     kspace = kspace_vectors.shape[1]
     norm_scale = 1.0 / math.sqrt(a_dev * n_atoms * kspace * kspace_tally)
 
-    pieces = 2
+    pieces = 4
     padded = jnp.concatenate([particle_coordinates, jnp.zeros((8 - particle_coordinates.shape[0], a_dev), F32)], axis=0)
     k_turns = (kspace_vectors * (0.5 / math.pi)).T
 
@@ -364,7 +364,7 @@
     places = (within // share) * count + (spatial_home // sub_rows) * share + within % share
     kvec_index = lax.axis_index("kvec")
 
-    k_part = kspace // pieces
+    k_part = kspace // 2
     made = {}
 
     def waves_of(half, n, k):

time: 243 us -> 277 us (1.14)
  the two profiles are of different devices: /device:TPU:23 before, /device:TPU:1 now
where the time goes in v3:
time: 277 us; the launch traced here: 276 us
  Pallas kernels  117 us (42%)
  starting transfers between devices  63.1 us (23%)
  waiting for transfers between devices  41.6 us (15%)
  local copies, waits for them, and re-layouts  37.6 us (14%)
  other arithmetic  14.9 us (5%)
    pallas_call x8, Pallas kernels, wave_sums(): pl.pallas_call(functools.partial(sums_kernel, min(512, a_dev)), grid=(ksp...  51.1 us
    ppermute x20, starting transfers between devices, shifted(): return lax.ppermute(array, 'atoms', pairs)  31.1 us
    pallas_call x1, Pallas kernels, edges(): pl.pallas_call(edges_kernel, grid=(e_dev // block,), in_specs=[scalars, s...  26.4 us
    all_to_all x4, starting transfers between devices, local(): lax.all_to_all(node, 'atoms', split_axis=0, concat_axis=0, tiled=True)  23.3 us
    pallas_call x4, Pallas kernels, update_rows(): pl.pallas_call(functools.partial(update_kernel, len(filts)), grid=(atoms...  21 us
    pallas_call x4, Pallas kernels, sort_atoms(): pl.pallas_call(functools.partial(sort_kernel, first), grid=(count // bloc...  18.7 us
    ppermute x10, waiting for transfers between devices, from_behind(): lax.ppermute(array, axis, [(i, (i + by) % devices) for i in range(devices)])  18.3 us
    unnamed x68, local copies, waits for them, and re-layouts  14.7 us
  transfers between devices with their start and end apart: 34, of which 15 were waited for; matrix products, arithmetic and copies ran while one was open for 8% of the time, Pallas kernels for 15%

profile of v3, /device:TPU:1, one launch (start us, length us, event | category | flops | bytes accessed | tf_op | source)
XLA Modules:
  0.0 276.5 jit_solution(2533014128390725762)
XLA Ops:
  4.1 4.7 %sort_atoms.4 = (bf16[1024,256]{1,0:T(8,128)(2,1)S(1)}, f32[8,1024]{1,0:T(8,128)S(1)}) custom-call(s32[1,4096]{1,0:T(1,128)S(1)} %fusion.ids_ref, f32[8,4096]{1,0:T(8,128)S(1)} %concatenate.6.coords_ref, bf16[4096,256]{1,0:T(8,128)(2,1)S(1)} %copy-done.22), custom_call_target="tpu_custom_call" | custom-call | flops 4294967296 | bytes 1048576 | tf_op jit(solution)/shard_map/sort_atoms/pallas_call | solution.py:67
  8.7 4.7 %sort_atoms.5 = (bf16[1024,256]{1,0:T(8,128)(2,1)S(1)}, f32[8,1024]{1,0:T(8,128)S(1)}) custom-call(s32[1,4096]{1,0:T(1,128)S(1)} %fusion.ids_ref, f32[8,4096]{1,0:T(8,128)S(1)} %concatenate.6.coords_ref, bf16[4096,256]{1,0:T(8,128)(2,1)S(1)} %copy-done.22), custom_call_target="tpu_custom_call" | custom-call | flops 4294967296 | bytes 1048576 | tf_op jit(solution)/shard_map/sort_atoms/pallas_call | solution.py:67
  13.5 4.7 %sort_atoms.6 = (bf16[1024,256]{1,0:T(8,128)(2,1)S(1)}, f32[8,1024]{1,0:T(8,128)S(1)}) custom-call(s32[1,4096]{1,0:T(1,128)S(1)} %fusion.ids_ref, f32[8,4096]{1,0:T(8,128)S(1)} %concatenate.6.coords_ref, bf16[4096,256]{1,0:T(8,128)(2,1)S(1)} %copy-done.22), custom_call_target="tpu_custom_call" | custom-call | flops 4294967296 | bytes 1048576 | tf_op jit(solution)/shard_map/sort_atoms/pallas_call | solution.py:67
  18.2 4.7 %sort_atoms.7 = (bf16[1024,256]{1,0:T(8,128)(2,1)S(1)}, f32[8,1024]{1,0:T(8,128)S(1)}) custom-call(s32[1,4096]{1,0:T(1,128)S(1)} %fusion.ids_ref, f32[8,4096]{1,0:T(8,128)S(1)} %concatenate.6.coords_ref, bf16[4096,256]{1,0:T(8,128)(2,1)S(1)} %copy-done.22), custom_call_target="tpu_custom_call" | custom-call | flops 4294967296 | bytes 1048576 | tf_op jit(solution)/shard_map/sort_atoms/pallas_call | solution.py:67
  23.3 6.4 %wave_sums.8 = (bf16[2,1024,256]{2,1,0:T(8,128)(2,1)S(1)}, bf16[1024,1024]{1,0:T(8,128)(2,1)S(1)}, bf16[1024,1024]{1,0:T(8,128)(2,1)}) custom-call(f32[1024,3]{1,0:T(8,128)S(1)} %slice.27.k_ref, f32[8,1024]{1,0:T(8,128)S(1)} %get-tuple-element.77.x_ref, bf16[1024,256]{1,0:T(8,128)(2,1)S(1)} %get-tuple-element.76.feat_ref), custom_call_target="tpu_custom_call" | custom-call | flops 2684354560 | bytes 1048576 | tf_op jit(solution)/shard_map/wave_sums/pallas_call | solution.py:123
  31.0 6.4 %wave_sums.9 = (bf16[2,1024,256]{2,1,0:T(8,128)(2,1)S(1)}, bf16[1024,1024]{1,0:T(8,128)(2,1)S(1)}, bf16[1024,1024]{1,0:T(8,128)(2,1)}) custom-call(f32[1024,3]{1,0:T(8,128)S(1)} %slice.27.k_ref, f32[8,1024]{1,0:T(8,128)S(1)} %get-tuple-element.79.x_ref, bf16[1024,256]{1,0:T(8,128)(2,1)S(1)} %get-tuple-element.80.feat_ref), custom_call_target="tpu_custom_call" | custom-call | flops 2684354560 | bytes 1048576 | tf_op jit(solution)/shard_map/wave_sums/pallas_call | solution.py:123
  38.8 6.4 %wave_sums.10 = (bf16[2,1024,256]{2,1,0:T(8,128)(2,1)S(1)}, bf16[1024,1024]{1,0:T(8,128)(2,1)S(1)}, bf16[1024,1024]{1,0:T(8,128)(2,1)}) custom-call(f32[1024,3]{1,0:T(8,128)S(1)} %slice.27.k_ref, f32[8,1024]{1,0:T(8,128)S(1)} %get-tuple-element.82.x_ref, bf16[1024,256]{1,0:T(8,128)(2,1)S(1)} %get-tuple-element.83.feat_ref), custom_call_target="tpu_custom_call" | custom-call | flops 2684354560 | bytes 1048576 | tf_op jit(solution)/shard_map/wave_sums/pallas_call | solution.py:123
  46.6 6.4 %wave_sums.11 = (bf16[2,1024,256]{2,1,0:T(8,128)(2,1)S(1)}, bf16[1024,1024]{1,0:T(8,128)(2,1)S(1)}, bf16[1024,1024]{1,0:T(8,128)(2,1)}) custom-call(f32[1024,3]{1,0:T(8,128)S(1)} %slice.27.k_ref, f32[8,1024]{1,0:T(8,128)S(1)} %get-tuple-element.85.x_ref, bf16[1024,256]{1,0:T(8,128)(2,1)S(1)} %get-tuple-element.86.feat_ref), custom_call_target="tpu_custom_call" | custom-call | flops 2684354560 | bytes 1048576 | tf_op jit(solution)/shard_map/wave_sums/pallas_call | solution.py:123
  59.6 6.4 %wave_sums.12 = (bf16[2,1024,256]{2,1,0:T(8,128)(2,1)S(1)}, bf16[1024,1024]{1,0:T(8,128)(2,1)S(1)}, bf16[1024,1024]{1,0:T(8,128)(2,1)}) custom-call(f32[1024,3]{1,0:T(8,128)S(1)} %copy-done.16, f32[8,1024]{1,0:T(8,128)S(1)} %get-tuple-element.77.x_ref, bf16[1024,256]{1,0:T(8,128)(2,1)S(1)} %get-tuple-element.76.feat_ref), custom_call_target="tpu_custom_call" | custom-call | flops 2684354560 | bytes 1048576 | tf_op jit(solution)/shard_map/wave_sums/pallas_call | solution.py:123
  68.5 2.8 collective-permute-start.1
  73.9 6.4 %wave_sums.13 = (bf16[2,1024,256]{2,1,0:T(8,128)(2,1)S(1)}, bf16[1024,1024]{1,0:T(8,128)(2,1)S(1)}, bf16[1024,1024]{1,0:T(8,128)(2,1)}) custom-call(f32[1024,3]{1,0:T(8,128)S(1)} %slice.20.k_ref, f32[8,1024]{1,0:T(8,128)S(1)} %get-tuple-element.79.x_ref, bf16[1024,256]{1,0:T(8,128)(2,1)S(1)} %get-tuple-element.80.feat_ref), custom_call_target="tpu_custom_call" | custom-call | flops 2684354560 | bytes 1048576 | tf_op jit(solution)/shard_map/wave_sums/pallas_call | solution.py:123
  86.3 6.4 %wave_sums.14 = (bf16[2,1024,256]{2,1,0:T(8,128)(2,1)S(1)}, bf16[1024,1024]{1,0:T(8,128)(2,1)S(1)}, bf16[1024,1024]{1,0:T(8,128)(2,1)}) custom-call(f32[1024,3]{1,0:T(8,128)S(1)} %slice.21.k_ref, f32[8,1024]{1,0:T(8,128)S(1)} %get-tuple-element.82.x_ref, bf16[1024,256]{1,0:T(8,128)(2,1)S(1)} %get-tuple-element.83.feat_ref), custom_call_target="tpu_custom_call" | custom-call | flops 2684354560 | bytes 1048576 | tf_op jit(solution)/shard_map/wave_sums/pallas_call | solution.py:123
  94.7 2.8 %collective-permute-start.7 = (bf16[2,64,256]{2,1,0:T(8,128)(2,1)S(1)}, bf16[2,64,256]{2,1,0:T(8,128)(2,1)S(1)}, u32[]{:S(2)}, u32[]{:S(2)}) collective-permute-start(bf16[2,64,256]{2,1,0:T(8,128)(2,1)S(1)} %multiply_convert_fusion.5), channel_id=1, source_target_pairs={{0,24},{2,26},{4,28},{6,30},{8,0},{10,2},{12,4},{14,6},{16,8},{18,... | collective-permute-start | bytes 196616 | tf_op jit(solution)/shard_map/ppermute | solution.py:272
  97.5 6.4 %wave_sums.15 = (bf16[2,1024,256]{2,1,0:T(8,128)(2,1)S(1)}, bf16[1024,1024]{1,0:T(8,128)(2,1)S(1)}, bf16[1024,1024]{1,0:T(8,128)(2,1)}) custom-call(f32[1024,3]{1,0:T(8,128)S(1)} %slice.22.k_ref, f32[8,1024]{1,0:T(8,128)S(1)} %get-tuple-element.85.x_ref, bf16[1024,256]{1,0:T(8,128)(2,1)S(1)} %get-tuple-element.86.feat_ref), custom_call_target="tpu_custom_call" | custom-call | flops 2684354560 | bytes 1048576 | tf_op jit(solution)/shard_map/wave_sums/pallas_call | solution.py:123
  109.0 7.3 %collective-permute-done.11 = bf16[2,256,256]{2,1,0:T(8,128)(2,1)S(1)} collective-permute-done((bf16[2,256,256]{2,1,0:T(8,128)(2,1)S(1)}, bf16[2,256,256]{2,1,0:T(8,128)(2,1)S(1)}, u32[]{:S(2)}, u32[]{:S(2)}) %collective-permute-start.11) | collective-permute-done | bytes 262176 | tf_op jit(solution)/shard_map/ppermute | solution.py:272
  122.6 3.2 %collective-permute-start.15 = (bf16[2,64,256]{2,1,0:T(8,128)(2,1)S(1)}, bf16[2,64,256]{2,1,0:T(8,128)(2,1)S(1)}, u32[]{:S(2)}, u32[]{:S(2)}) collective-permute-start(bf16[2,64,256]{2,1,0:T(8,128)(2,1)S(1)} %get-tuple-element.151), channel_id=1, source_target_pairs={{0,8},{2,10},{4,12},{6,14},{8,16},{10,18},{12,20},{14,22},{16,24},... | collective-permute-start | bytes 196616 | tf_op jit(solution)/shard_map/ppermute | solution.py:272
  133.0 3.2 %collective-permute-start.9 = (bf16[2,512,256]{2,1,0:T(8,128)(2,1)S(1)}, bf16[2,512,256]{2,1,0:T(8,128)(2,1)S(1)}, u32[]{:S(2)}, u32[]{:S(2)}) collective-permute-start(bf16[2,512,256]{2,1,0:T(8,128)(2,1)S(1)} %constant_dynamic-update-slice_fusion.10), channel_id=1, source_target_pairs={{0,2},{2,0},{4,6},{6,4},{8,10},{10,8},{12,14},{14,12},{16,18},{18,... | collective-permute-start | bytes 1572872 | tf_op jit(solution)/shard_map/ppermute | solution.py:272
  138.5 3.4 %collective-permute-start.19 = (bf16[2,512,256]{2,1,0:T(8,128)(2,1)}, bf16[2,512,256]{2,1,0:T(8,128)(2,1)}, u32[]{:S(2)}, u32[]{:S(2)}) collective-permute-start(bf16[2,512,256]{2,1,0:T(8,128)(2,1)} %constant_dynamic-update-slice_fusion.2), channel_id=1, source_target_pairs={{0,2},{2,0},{4,6},{6,4},{8,10},{10,8},{12,14},{14,12},{16,18},{18,... | collective-permute-start | bytes 1572872 | tf_op jit(solution)/shard_map/ppermute | solution.py:272
  144.9 5.4 %update_rows.4 = bf16[1024,256]{1,0:T(8,128)(2,1)S(1)} custom-call(bf16[2,1024,256]{2,1,0:T(8,128)(2,1)S(1)} %constant_dynamic-update-slice_fusion.8.refs_0_, bf16[2,1024,256]{2,1,0:T(8,128)(2,1)S(1)} %constant_dynamic-update-slice_fusion.refs_1_, bf16[1024,1024]{1,0:T(8,128)(2,1)S(1)} %copy-done.8, bf16[1024,1024]{1,0:T(8,128)(2,1)} %get-tuple-element.120.refs_3_, ...), custom_call_target="tpu_custom_call" | custom-call | flops 2147483648 | bytes 8388608 | tf_op jit(solution)/shard_map/update_rows/pallas_call | solution.py:166
  151.6 5.3 %update_rows.5 = bf16[1024,256]{1,0:T(8,128)(2,1)S(1)} custom-call(bf16[2,1024,256]{2,1,0:T(8,128)(2,1)S(1)} %constant_dynamic-update-slice_fusion.8.refs_0_, bf16[2,1024,256]{2,1,0:T(8,128)(2,1)S(1)} %constant_dynamic-update-slice_fusion.refs_1_, bf16[1024,1024]{1,0:T(8,128)(2,1)S(1)} %copy-done.6, bf16[1024,1024]{1,0:T(8,128)(2,1)} %get-tuple-element.124.refs_3_, ...), custom_call_target="tpu_custom_call" | custom-call | flops 2147483648 | bytes 8388608 | tf_op jit(solution)/shard_map/update_rows/pallas_call | solution.py:166
  159.1 5.5 %all-to-all-start = ((bf16[16,32,256]{2,1,0:T(8,128)(2,1)}), bf16[16,32,256]{2,1,0:T(8,128)(2,1)}, u32[]{:S(2)}, u32[]{:S(2)}) async-start(bf16[16,32,256]{2,1,0:T(8,128)(2,1)} %multiply_convert_fusion.3), calls=%async_computation | async-start | bytes 524288 | tf_op jit(solution)/shard_map/all_to_all | solution.py:421
  167.5 5.2 %update_rows.6 = bf16[1024,256]{1,0:T(8,128)(2,1)S(1)} custom-call(bf16[2,1024,256]{2,1,0:T(8,128)(2,1)S(1)} %constant_dynamic-update-slice_fusion.8.refs_0_, bf16[2,1024,256]{2,1,0:T(8,128)(2,1)S(1)} %constant_dynamic-update-slice_fusion.refs_1_, bf16[1024,1024]{1,0:T(8,128)(2,1)S(1)} %copy-done.4, bf16[1024,1024]{1,0:T(8,128)(2,1)} %get-tuple-element.131.refs_3_, ...), custom_call_target="tpu_custom_call" | custom-call | flops 2147483648 | bytes 8388608 | tf_op jit(solution)/shard_map/update_rows/pallas_call | solution.py:166
  177.7 5.5 %all-to-all-start.1 = ((bf16[16,32,256]{2,1,0:T(8,128)(2,1)}), bf16[16,32,256]{2,1,0:T(8,128)(2,1)}, u32[]{:S(2)}, u32[]{:S(2)}) async-start(bf16[16,32,256]{2,1,0:T(8,128)(2,1)} %multiply_convert_fusion.2), calls=%async_computation.1 | async-start | bytes 524288 | tf_op jit(solution)/shard_map/all_to_all | solution.py:421
  185.8 5.2 %update_rows.7 = bf16[1024,256]{1,0:T(8,128)(2,1)S(1)} custom-call(bf16[2,1024,256]{2,1,0:T(8,128)(2,1)S(1)} %constant_dynamic-update-slice_fusion.8.refs_0_, bf16[2,1024,256]{2,1,0:T(8,128)(2,1)S(1)} %constant_dynamic-update-slice_fusion.refs_1_, bf16[1024,1024]{1,0:T(8,128)(2,1)S(1)} %copy-done.2, bf16[1024,1024]{1,0:T(8,128)(2,1)} %get-tuple-element.140.refs_3_, ...), custom_call_target="tpu_custom_call" | custom-call | flops 2147483648 | bytes 8388608 | tf_op jit(solution)/shard_map/update_rows/pallas_call | solution.py:166
  196.0 6.3 %all-to-all-start.2 = ((bf16[16,32,256]{2,1,0:T(8,128)(2,1)}), bf16[16,32,256]{2,1,0:T(8,128)(2,1)S(1)}, u32[]{:S(2)}, u32[]{:S(2)}) async-start(bf16[16,32,256]{2,1,0:T(8,128)(2,1)} %multiply_convert_fusion.1), calls=%async_computation.2 | async-start | bytes 524288 | tf_op jit(solution)/shard_map/all_to_all | solution.py:421
  206.2 4.3 %collective-permute-done.26 = bf16[16,32,256]{2,1,0:T(8,128)(2,1)S(1)} collective-permute-done((bf16[16,32,256]{2,1,0:T(8,128)(2,1)}, bf16[16,32,256]{2,1,0:T(8,128)(2,1)S(1)}, u32[]{:S(2)}, u32[]{:S(2)}) %collective-permute-start.26) | collective-permute-done | bytes 262176 | tf_op jit(solution)/shard_map/ppermute | solution.py:253
  213.0 6.0 %all-to-all-start.3 = ((bf16[16,32,256]{2,1,0:T(8,128)(2,1)}), bf16[16,32,256]{2,1,0:T(8,128)(2,1)S(1)}, u32[]{:S(2)}, u32[]{:S(2)}) async-start(bf16[16,32,256]{2,1,0:T(8,128)(2,1)} %multiply_convert_fusion), calls=%async_computation.3 | async-start | bytes 524288 | tf_op jit(solution)/shard_map/all_to_all | solution.py:421
  221.7 6.8 %all-to-all-done.3 = bf16[16,32,256]{2,1,0:T(8,128)(2,1)S(1)} async-done(((bf16[16,32,256]{2,1,0:T(8,128)(2,1)}), bf16[16,32,256]{2,1,0:T(8,128)(2,1)S(1)}, u32[]{:S(2)}, u32[]{:S(2)}) %all-to-all-start.3) | async-done | bytes 262176 | tf_op jit(solution)/shard_map/all_to_all | solution.py:421
  229.2 6.5 %collective-permute-done.27 = bf16[16,32,256]{2,1,0:T(8,128)(2,1)S(1)} collective-permute-done((bf16[16,32,256]{2,1,0:T(8,128)(2,1)S(1)}, bf16[16,32,256]{2,1,0:T(8,128)(2,1)S(1)}, u32[]{:S(2)}, u32[]{:S(2)}) %collective-permute-start.27) | collective-permute-done | bytes 262176 | tf_op jit(solution)/shard_map/ppermute | solution.py:253
  239.3 2.6 gather_fusion.1
  242.6 7.3 %collective-permute-done.29 = bf16[512,256]{1,0:T(8,128)(2,1)S(1)} collective-permute-done((bf16[512,256]{1,0:T(8,128)(2,1)}, bf16[512,256]{1,0:T(8,128)(2,1)S(1)}, u32[]{:S(2)}, u32[]{:S(2)}) %collective-permute-start.29) | collective-permute-done | bytes 262176 | tf_op jit(solution)/shard_map/ppermute | solution.py:253
  250.1 26.4 %edges.1 = bf16[196,4096]{1,0:T(8,128)(2,1)} custom-call(s32[4096]{0:T(1024)S(1)} %copy-done.20, s32[4096]{0:T(1024)S(1)} %copy-done.21, s32[1]{0:T(128)S(6)} %copy.82.used_ref, bf16[5120,256]{1,0:T(8,128)(2,1)S(1)} %pad_maximum_fusion.table_ref, bf16[4096,256]{1,0:T(8,128)(2,1)S(1)} %bitcast.101, bf16[256,256]{1,0:T(8,128)(2,1)S(1)} %copy-done.17, ...), custom_call_target="tpu_custom_call" | custom-call | tf_op jit(solution)/shard_map/edges/pallas_call | solution.py:235
  (197 shorter events, 83.8 us)
Async XLA Ops:
  57.6 9.7 %collective-permute-start = (bf16[2,512,256]{2,1,0:T(8,128)(2,1)}, bf16[2,512,256]{2,1,0:T(8,128)(2,1)}, u32[]{:S(2)}, u32[]{:S(2)}) collective-permute-start(bf16[2,512,256]{2,1,0:T(8,128)(2,1)} %constant_dynamic-slice_fusion.10), channel_id=1, source_target_pairs={{0,2},{2,0},{4,6},{6,4},{8,10},{10,8},{12,14},{14,12},{16,18},{18,... | collective-permute-start | bytes 1572872 | tf_op jit(solution)/shard_map/ppermute | solution.py:272
  68.5 11.8 %collective-permute-start.1 = (bf16[2,256,256]{2,1,0:T(8,128)(2,1)S(1)}, bf16[2,256,256]{2,1,0:T(8,128)(2,1)}, u32[]{:S(2)}, u32[]{:S(2)}) collective-permute-start(bf16[2,256,256]{2,1,0:T(8,128)(2,1)S(1)} %constant_dynamic-slice_fusion.9), channel_id=1, source_target_pairs={{0,4},{2,6},{4,0},{6,2},{8,12},{10,14},{12,8},{14,10},{16,20},{18,... | collective-permute-start | bytes 786440 | tf_op jit(solution)/shard_map/ppermute | solution.py:272
  81.6 12.5 %collective-permute-start.2 = (bf16[2,64,256]{2,1,0:T(8,128)(2,1)S(1)}, bf16[2,64,256]{2,1,0:T(8,128)(2,1)S(1)}, u32[]{:S(2)}, u32[]{:S(2)}) collective-permute-start(bf16[2,64,256]{2,1,0:T(8,128)(2,1)S(1)} %get-tuple-element.165), channel_id=1, source_target_pairs={{0,8},{2,10},{4,12},{6,14},{8,16},{10,18},{12,20},{14,22},{16,24},... | collective-permute-start | bytes 196616 | tf_op jit(solution)/shard_map/ppermute | solution.py:272
  82.9 11.1 %collective-permute-start.3 = (bf16[2,64,256]{2,1,0:T(8,128)(2,1)S(1)}, bf16[2,64,256]{2,1,0:T(8,128)(2,1)S(1)}, u32[]{:S(2)}, u32[]{:S(2)}) collective-permute-start(bf16[2,64,256]{2,1,0:T(8,128)(2,1)S(1)} %get-tuple-element.167), channel_id=1, source_target_pairs={{0,16},{2,18},{4,20},{6,22},{8,24},{10,26},{12,28},{14,30},{16,0},... | collective-permute-start | bytes 196616 | tf_op jit(solution)/shard_map/ppermute | solution.py:272
  85.3 8.8 %collective-permute-start.4 = (bf16[2,64,256]{2,1,0:T(8,128)(2,1)S(1)}, bf16[2,64,256]{2,1,0:T(8,128)(2,1)S(1)}, u32[]{:S(2)}, u32[]{:S(2)}) collective-permute-start(bf16[2,64,256]{2,1,0:T(8,128)(2,1)S(1)} %get-tuple-element.166), channel_id=1, source_target_pairs={{0,24},{2,26},{4,28},{6,30},{8,0},{10,2},{12,4},{14,6},{16,8},{18,... | collective-permute-start | bytes 196616 | tf_op jit(solution)/shard_map/ppermute | solution.py:272
  94.1 9.8 %collective-permute-start.5 = (bf16[2,64,256]{2,1,0:T(8,128)(2,1)S(1)}, bf16[2,64,256]{2,1,0:T(8,128)(2,1)S(1)}, u32[]{:S(2)}, u32[]{:S(2)}) collective-permute-start(bf16[2,64,256]{2,1,0:T(8,128)(2,1)S(1)} %multiply_convert_fusion.5), channel_id=1, source_target_pairs={{0,8},{2,10},{4,12},{6,14},{8,16},{10,18},{12,20},{14,22},{16,24},... | collective-permute-start | bytes 196616 | tf_op jit(solution)/shard_map/ppermute | solution.py:272
  94.6 9.4 %collective-permute-start.6 = (bf16[2,64,256]{2,1,0:T(8,128)(2,1)S(1)}, bf16[2,64,256]{2,1,0:T(8,128)(2,1)S(1)}, u32[]{:S(2)}, u32[]{:S(2)}) collective-permute-start(bf16[2,64,256]{2,1,0:T(8,128)(2,1)S(1)} %multiply_convert_fusion.5), channel_id=1, source_target_pairs={{0,16},{2,18},{4,20},{6,22},{8,24},{10,26},{12,28},{14,30},{16,0},... | collective-permute-start | bytes 196616 | tf_op jit(solution)/shard_map/ppermute | solution.py:272
  94.7 9.4 %collective-permute-start.7 = (bf16[2,64,256]{2,1,0:T(8,128)(2,1)S(1)}, bf16[2,64,256]{2,1,0:T(8,128)(2,1)S(1)}, u32[]{:S(2)}, u32[]{:S(2)}) collective-permute-start(bf16[2,64,256]{2,1,0:T(8,128)(2,1)S(1)} %multiply_convert_fusion.5), channel_id=1, source_target_pairs={{0,24},{2,26},{4,28},{6,30},{8,0},{10,2},{12,4},{14,6},{16,8},{18,... | collective-permute-start | bytes 196616 | tf_op jit(solution)/shard_map/ppermute | solution.py:272
  108.7 7.6 %collective-permute-start.11 = (bf16[2,256,256]{2,1,0:T(8,128)(2,1)S(1)}, bf16[2,256,256]{2,1,0:T(8,128)(2,1)S(1)}, u32[]{:S(2)}, u32[]{:S(2)}) collective-permute-start(bf16[2,256,256]{2,1,0:T(8,128)(2,1)S(1)} %constant_dynamic-slice_fusion.3), channel_id=1, source_target_pairs={{0,4},{2,6},{4,0},{6,2},{8,12},{10,14},{12,8},{14,10},{16,20},{18,... | collective-permute-start | bytes 786440 | tf_op jit(solution)/shard_map/ppermute | solution.py:272
  116.4 5.1 %collective-permute-start.12 = (bf16[2,64,256]{2,1,0:T(8,128)(2,1)S(1)}, bf16[2,64,256]{2,1,0:T(8,128)(2,1)S(1)}, u32[]{:S(2)}, u32[]{:S(2)}) collective-permute-start(bf16[2,64,256]{2,1,0:T(8,128)(2,1)S(1)} %get-tuple-element.162), channel_id=1, source_target_pairs={{0,8},{2,10},{4,12},{6,14},{8,16},{10,18},{12,20},{14,22},{16,24},... | collective-permute-start | bytes 196616 | tf_op jit(solution)/shard_map/ppermute | solution.py:272
  116.8 4.8 %collective-permute-start.13 = (bf16[2,64,256]{2,1,0:T(8,128)(2,1)S(1)}, bf16[2,64,256]{2,1,0:T(8,128)(2,1)S(1)}, u32[]{:S(2)}, u32[]{:S(2)}) collective-permute-start(bf16[2,64,256]{2,1,0:T(8,128)(2,1)S(1)} %get-tuple-element.164), channel_id=1, source_target_pairs={{0,16},{2,18},{4,20},{6,22},{8,24},{10,26},{12,28},{14,30},{16,0},... | collective-permute-start | bytes 196616 | tf_op jit(solution)/shard_map/ppermute | solution.py:272
  122.6 5.6 %collective-permute-start.15 = (bf16[2,64,256]{2,1,0:T(8,128)(2,1)S(1)}, bf16[2,64,256]{2,1,0:T(8,128)(2,1)S(1)}, u32[]{:S(2)}, u32[]{:S(2)}) collective-permute-start(bf16[2,64,256]{2,1,0:T(8,128)(2,1)S(1)} %get-tuple-element.151), channel_id=1, source_target_pairs={{0,8},{2,10},{4,12},{6,14},{8,16},{10,18},{12,20},{14,22},{16,24},... | collective-permute-start | bytes 196616 | tf_op jit(solution)/shard_map/ppermute | solution.py:272
  125.8 7.2 %collective-permute-start.8 = (bf16[2,256,256]{2,1,0:T(8,128)(2,1)S(1)}, bf16[2,256,256]{2,1,0:T(8,128)(2,1)S(1)}, u32[]{:S(2)}, u32[]{:S(2)}) collective-permute-start(bf16[2,256,256]{2,1,0:T(8,128)(2,1)S(1)} %constant_dynamic-update-slice_fusion.12), channel_id=1, source_target_pairs={{0,4},{2,6},{4,0},{6,2},{8,12},{10,14},{12,8},{14,10},{16,20},{18,... | collective-permute-start | bytes 786440 | tf_op jit(solution)/shard_map/ppermute | solution.py:272
  126.0 4.6 %collective-permute-start.16 = (bf16[2,64,256]{2,1,0:T(8,128)(2,1)S(1)}, bf16[2,64,256]{2,1,0:T(8,128)(2,1)S(1)}, u32[]{:S(2)}, u32[]{:S(2)}) collective-permute-start(bf16[2,64,256]{2,1,0:T(8,128)(2,1)S(1)} %get-tuple-element.151), channel_id=1, source_target_pairs={{0,16},{2,18},{4,20},{6,22},{8,24},{10,26},{12,28},{14,30},{16,0},... | collective-permute-start | bytes 196616 | tf_op jit(solution)/shard_map/ppermute | solution.py:272
  126.8 4.2 %collective-permute-start.17 = (bf16[2,64,256]{2,1,0:T(8,128)(2,1)S(1)}, bf16[2,64,256]{2,1,0:T(8,128)(2,1)S(1)}, u32[]{:S(2)}, u32[]{:S(2)}) collective-permute-start(bf16[2,64,256]{2,1,0:T(8,128)(2,1)S(1)} %get-tuple-element.151), channel_id=1, source_target_pairs={{0,24},{2,26},{4,28},{6,30},{8,0},{10,2},{12,4},{14,6},{16,8},{18,... | collective-permute-start | bytes 196616 | tf_op jit(solution)/shard_map/ppermute | solution.py:272
  131.1 6.8 %collective-permute-start.18 = (bf16[2,256,256]{2,1,0:T(8,128)(2,1)S(1)}, bf16[2,256,256]{2,1,0:T(8,128)(2,1)S(1)}, u32[]{:S(2)}, u32[]{:S(2)}) collective-permute-start(bf16[2,256,256]{2,1,0:T(8,128)(2,1)S(1)} %constant_dynamic-update-slice_fusion.4), channel_id=1, source_target_pairs={{0,4},{2,6},{4,0},{6,2},{8,12},{10,14},{12,8},{14,10},{16,20},{18,... | collective-permute-start | bytes 786440 | tf_op jit(solution)/shard_map/ppermute | solution.py:272
  133.0 9.0 %collective-permute-start.9 = (bf16[2,512,256]{2,1,0:T(8,128)(2,1)S(1)}, bf16[2,512,256]{2,1,0:T(8,128)(2,1)S(1)}, u32[]{:S(2)}, u32[]{:S(2)}) collective-permute-start(bf16[2,512,256]{2,1,0:T(8,128)(2,1)S(1)} %constant_dynamic-update-slice_fusion.10), channel_id=1, source_target_pairs={{0,2},{2,0},{4,6},{6,4},{8,10},{10,8},{12,14},{14,12},{16,18},{18,... | collective-permute-start | bytes 1572872 | tf_op jit(solution)/shard_map/ppermute | solution.py:272
  138.5 5.2 %collective-permute-start.19 = (bf16[2,512,256]{2,1,0:T(8,128)(2,1)}, bf16[2,512,256]{2,1,0:T(8,128)(2,1)}, u32[]{:S(2)}, u32[]{:S(2)}) collective-permute-start(bf16[2,512,256]{2,1,0:T(8,128)(2,1)} %constant_dynamic-update-slice_fusion.2), channel_id=1, source_target_pairs={{0,2},{2,0},{4,6},{6,4},{8,10},{10,8},{12,14},{14,12},{16,18},{18,... | collective-permute-start | bytes 1572872 | tf_op jit(solution)/shard_map/ppermute | solution.py:272
  150.3 7.6 %collective-permute-start.20 = (bf16[16,32,256]{2,1,0:T(8,128)(2,1)S(1)}, bf16[16,32,256]{2,1,0:T(8,128)(2,1)S(1)}, u32[]{:S(2)}, u32[]{:S(2)}) collective-permute-start(bf16[16,32,256]{2,1,0:T(8,128)(2,1)S(1)} %get-tuple-element.160), channel_id=1, source_target_pairs={{0,1},{1,0},{2,3},{3,2},{4,5},{5,4},{6,7},{7,6},{8,9},{9,8},{10,11... | collective-permute-start | bytes 786440 | tf_op jit(solution)/shard_map/ppermute | solution.py:253
  159.1 15.1 %all-to-all-start = ((bf16[16,32,256]{2,1,0:T(8,128)(2,1)}), bf16[16,32,256]{2,1,0:T(8,128)(2,1)}, u32[]{:S(2)}, u32[]{:S(2)}) async-start(bf16[16,32,256]{2,1,0:T(8,128)(2,1)} %multiply_convert_fusion.3), calls=%async_computation | async-start | bytes 524288 | tf_op jit(solution)/shard_map/all_to_all | solution.py:421
  164.6 8.8 %collective-permute-start.22 = (bf16[16,32,256]{2,1,0:T(8,128)(2,1)}, bf16[16,32,256]{2,1,0:T(8,128)(2,1)}, u32[]{:S(2)}, u32[]{:S(2)}) collective-permute-start(bf16[16,32,256]{2,1,0:T(8,128)(2,1)} %get-tuple-element.158), channel_id=1, source_target_pairs={{0,1},{1,0},{2,3},{3,2},{4,5},{5,4},{6,7},{7,6},{8,9},{9,8},{10,11... | collective-permute-start | bytes 786440 | tf_op jit(solution)/shard_map/ppermute | solution.py:253
  177.7 15.1 %all-to-all-start.1 = ((bf16[16,32,256]{2,1,0:T(8,128)(2,1)}), bf16[16,32,256]{2,1,0:T(8,128)(2,1)}, u32[]{:S(2)}, u32[]{:S(2)}) async-start(bf16[16,32,256]{2,1,0:T(8,128)(2,1)} %multiply_convert_fusion.2), calls=%async_computation.1 | async-start | bytes 524288 | tf_op jit(solution)/shard_map/all_to_all | solution.py:421
  183.3 8.4 %collective-permute-start.24 = (bf16[16,32,256]{2,1,0:T(8,128)(2,1)}, bf16[16,32,256]{2,1,0:T(8,128)(2,1)}, u32[]{:S(2)}, u32[]{:S(2)}) collective-permute-start(bf16[16,32,256]{2,1,0:T(8,128)(2,1)} %get-tuple-element.156), channel_id=1, source_target_pairs={{0,1},{1,0},{2,3},{3,2},{4,5},{5,4},{6,7},{7,6},{8,9},{9,8},{10,11... | collective-permute-start | bytes 786440 | tf_op jit(solution)/shard_map/ppermute | solution.py:253
  191.7 12.5 %collective-permute-start.21 = (bf16[16,32,256]{2,1,0:T(8,128)(2,1)}, bf16[16,32,256]{2,1,0:T(8,128)(2,1)}, u32[]{:S(2)}, u32[]{:S(2)}) collective-permute-start(bf16[16,32,256]{2,1,0:T(8,128)(2,1)} %all-to-all-done), channel_id=1, source_target_pairs={{0,1},{1,0},{2,3},{3,2},{4,5},{5,4},{6,7},{7,6},{8,9},{9,8},{10,11... | collective-permute-start | bytes 786440 | tf_op jit(solution)/shard_map/ppermute | solution.py:253
  196.0 15.8 %all-to-all-start.2 = ((bf16[16,32,256]{2,1,0:T(8,128)(2,1)}), bf16[16,32,256]{2,1,0:T(8,128)(2,1)S(1)}, u32[]{:S(2)}, u32[]{:S(2)}) async-start(bf16[16,32,256]{2,1,0:T(8,128)(2,1)} %multiply_convert_fusion.1), calls=%async_computation.2 | async-start | bytes 524288 | tf_op jit(solution)/shard_map/all_to_all | solution.py:421
  202.3 8.1 %collective-permute-start.26 = (bf16[16,32,256]{2,1,0:T(8,128)(2,1)}, bf16[16,32,256]{2,1,0:T(8,128)(2,1)S(1)}, u32[]{:S(2)}, u32[]{:S(2)}) collective-permute-start(bf16[16,32,256]{2,1,0:T(8,128)(2,1)} %get-tuple-element.154), channel_id=1, source_target_pairs={{0,1},{1,0},{2,3},{3,2},{4,5},{5,4},{6,7},{7,6},{8,9},{9,8},{10,11... | collective-permute-start | bytes 786440 | tf_op jit(solution)/shard_map/ppermute | solution.py:253
  205.3 15.4 %collective-permute-start.23 = (bf16[16,32,256]{2,1,0:T(8,128)(2,1)}, bf16[16,32,256]{2,1,0:T(8,128)(2,1)}, u32[]{:S(2)}, u32[]{:S(2)}) collective-permute-start(bf16[16,32,256]{2,1,0:T(8,128)(2,1)} %all-to-all-done.1), channel_id=1, source_target_pairs={{0,1},{1,0},{2,3},{3,2},{4,5},{5,4},{6,7},{7,6},{8,9},{9,8},{10,11... | collective-permute-start | bytes 786440 | tf_op jit(solution)/shard_map/ppermute | solution.py:253
  213.0 15.5 %all-to-all-start.3 = ((bf16[16,32,256]{2,1,0:T(8,128)(2,1)}), bf16[16,32,256]{2,1,0:T(8,128)(2,1)S(1)}, u32[]{:S(2)}, u32[]{:S(2)}) async-start(bf16[16,32,256]{2,1,0:T(8,128)(2,1)} %multiply_convert_fusion), calls=%async_computation.3 | async-start | bytes 524288 | tf_op jit(solution)/shard_map/all_to_all | solution.py:421
  220.0 9.2 %collective-permute-start.25 = (bf16[16,32,256]{2,1,0:T(8,128)(2,1)S(1)}, bf16[16,32,256]{2,1,0:T(8,128)(2,1)S(1)}, u32[]{:S(2)}, u32[]{:S(2)}) collective-permute-start(bf16[16,32,256]{2,1,0:T(8,128)(2,1)S(1)} %all-to-all-done.2), channel_id=1, source_target_pairs={{0,1},{1,0},{2,3},{3,2},{4,5},{5,4},{6,7},{7,6},{8,9},{9,8},{10,11... | collective-permute-start | bytes 786440 | tf_op jit(solution)/shard_map/ppermute | solution.py:253
  228.5 7.2 %collective-permute-start.27 = (bf16[16,32,256]{2,1,0:T(8,128)(2,1)S(1)}, bf16[16,32,256]{2,1,0:T(8,128)(2,1)S(1)}, u32[]{:S(2)}, u32[]{:S(2)}) collective-permute-start(bf16[16,32,256]{2,1,0:T(8,128)(2,1)S(1)} %all-to-all-done.3), channel_id=1, source_target_pairs={{0,1},{1,0},{2,3},{3,2},{4,5},{5,4},{6,7},{7,6},{8,9},{9,8},{10,11... | collective-permute-start | bytes 786440 | tf_op jit(solution)/shard_map/ppermute | solution.py:253
  237.7 4.9 %collective-permute-start.28 = (bf16[512,256]{1,0:T(8,128)(2,1)S(1)}, bf16[512,256]{1,0:T(8,128)(2,1)S(1)}, u32[]{:S(2)}, u32[]{:S(2)}) collective-permute-start(bf16[512,256]{1,0:T(8,128)(2,1)S(1)} %gather_fusion), channel_id=1, source_target_pairs={{0,2},{2,4},{4,6},{6,8},{8,10},{10,12},{12,14},{14,16},{16,18},{18... | collective-permute-start | bytes 786440 | tf_op jit(solution)/shard_map/ppermute | solution.py:253
  241.8 8.0 %collective-permute-start.29 = (bf16[512,256]{1,0:T(8,128)(2,1)}, bf16[512,256]{1,0:T(8,128)(2,1)S(1)}, u32[]{:S(2)}, u32[]{:S(2)}) collective-permute-start(bf16[512,256]{1,0:T(8,128)(2,1)} %gather_fusion.1), channel_id=1, source_target_pairs={{0,30},{2,0},{4,2},{6,4},{8,6},{10,8},{12,10},{14,12},{16,14},{18,... | collective-permute-start | bytes 786440 | tf_op jit(solution)/shard_map/ppermute | solution.py:253
  (36 other events, 324.8 us)
